TPU v7x, 32 devices: a whole 2x2x4 slice. The times are simulated.
32 devices in a mesh: grp: 4 (over x, core), mem: 8 (over z, y).
Axes of the slice: x: 2, y: 2, z: 4, core: 2. Of those that a mesh axis runs over, the one named last changes fastest.
Arguments:
- dec_input: bfloat16 [4, 4, 256, 1024], P('grp'), may hold values from -6 to 6
- memory: bfloat16 [4, 4, 512, 1024], P('grp', None, 'mem'), may hold values from -6 to 6
- out_grad: bfloat16 [4, 4, 256, 1024], P('grp'), may hold values from -6 to 6
- tgt_lengths: int32 [4, 4], P('grp'), may hold values from 128 to 256, as said below
- src_lengths: int32 [4, 4], P('grp'), may hold values from 64 to 512, as said below
- self_qkv: bfloat16 [3, 1024, 1024], replicated, may hold values from -0.1875 to 0.1875
- self_out: bfloat16 [1024, 1024], replicated, may hold values from -0.75 to 0.75
- cross_qkv: bfloat16 [3, 1024, 1024], replicated, may hold values from -0.1875 to 0.1875
- cross_out: bfloat16 [1024, 1024], replicated, may hold values from -1.5 to 1.5
- ffn_in: bfloat16 [1024, 4096], replicated, may hold values from -0.1875 to 0.1875
- ffn_out: bfloat16 [4096, 1024], replicated, may hold values from -0.09375 to 0.09375
- norm_gains: float32 [3, 1024], replicated, may hold values from 0.5 to 1.5
- norm_biases: float32 [3, 1024], replicated, may hold values from -1 to 1
- down_w: float32 [4, 1024, 512], P('grp', 'mem'), may hold values from -0.1875 to 0.1875
- up_w: float32 [4, 512, 1024], P('grp', 'mem'), may hold values from -0.0625 to 0.0625
- prefix_w: float32 [4, 2, 30, 1024], P('grp', None, None, 'mem'), may hold values from -5 to 5
- down_m: float32 [4, 1024, 512], P('grp', 'mem'), may hold values from -7.3161826 to 7.3161826
- down_v: float32 [4, 1024, 512], P('grp', 'mem'), may hold values from 0.27648 to 1.10592
- up_m: float32 [4, 512, 1024], P('grp', 'mem'), may hold values from -23.135801 to 23.135801
- up_v: float32 [4, 512, 1024], P('grp', 'mem'), may hold values from 2.7648 to 11.0592
- prefix_m: float32 [4, 2, 30, 1024], P('grp', None, None, 'mem'), may hold values from -0.21461475 to 0.21461475
- prefix_v: float32 [4, 2, 30, 1024], P('grp', None, None, 'mem'), may hold values from 0.00023791059 to 0.00095164235
- down_outer: float32 [1024, 512], P('mem'), may hold values from -0.1875 to 0.1875
- up_outer: float32 [512, 1024], P('mem'), may hold values from -0.0625 to 0.0625
- prefix_outer: float32 [2, 30, 1024], P(None, None, 'mem'), may hold values from -5 to 5
- down_mom: float32 [1024, 512], P('mem'), may hold values from -0.1875 to 0.1875
- up_mom: float32 [512, 1024], P('mem'), may hold values from -0.0625 to 0.0625
- prefix_mom: float32 [2, 30, 1024], P(None, None, 'mem'), may hold values from -5 to 5
Outputs:
- output: bfloat16 [4, 4, 256, 1024], P('grp')
- grad_input: float32 [4, 4, 256, 1024], P('grp')
- grad_memory: float32 [4, 4, 512, 1024], P('grp', None, 'mem')
- grad_down: float32 [4, 1024, 512], P('grp', 'mem')
- grad_up: float32 [4, 512, 1024], P('grp', 'mem')
- grad_prefix: float32 [4, 2, 30, 1024], P('grp', None, None, 'mem')
- new_down_m: float32 [4, 1024, 512], P('grp', 'mem')
- new_down_v: float32 [4, 1024, 512], P('grp', 'mem')
- new_down_w: float32 [4, 1024, 512], P('grp', 'mem')
- new_up_m: float32 [4, 512, 1024], P('grp', 'mem')
- new_up_v: float32 [4, 512, 1024], P('grp', 'mem')
- new_up_w: float32 [4, 512, 1024], P('grp', 'mem')
- new_prefix_m: float32 [4, 2, 30, 1024], P('grp', None, None, 'mem')
- new_prefix_v: float32 [4, 2, 30, 1024], P('grp', None, None, 'mem')
- new_prefix_w: float32 [4, 2, 30, 1024], P('grp', None, None, 'mem')
- new_down_mom: float32 [1024, 512], P('mem')
- new_down_outer: float32 [1024, 512], P('mem')
- new_up_mom: float32 [512, 1024], P('mem')
- new_up_outer: float32 [512, 1024], P('mem')
- new_prefix_mom: float32 [2, 30, 1024], P(None, None, 'mem')
- new_prefix_outer: float32 [2, 30, 1024], P(None, None, 'mem')
Inputs may be any that keep to these rules, and one draw needn't show every extreme that they name: `tgt_lengths`: in each group one sequence, drawn from the seed, has exactly 256. `src_lengths`: in each group one sequence, drawn from the seed, has exactly 512.
All inputs are finite; a program needn't handle non-finite values.
Results may differ from a plain program's by a relative error of at most 0.025.
Values may be sent and summed in bfloat16 or wider, within the bound.
No kernel may reach another device: no remote copies, remote signals or barrier semaphores. Data moves between devices by JAX's collectives and lax.ppermute only.
A program may use at most 256 MiB of HBM per device.

v0:
```python
import jax
import jax.numpy as jnp
from jax import lax
from jax.sharding import PartitionSpec as P

HEADS = 16
HDIM = 64
STEP = 10


EPSILON = 1e-05
NEGATIVE = -1e30
ADAPTER_SCALE = 4.0
OUTER_MOMENTUM = 0.9
OUTER_RATE = 0.7


def normalize(values_in, gain_row, bias_row):
    centered = values_in - jnp.mean(values_in, -1, keepdims=True)
    scale_inv = lax.rsqrt(jnp.mean(centered * centered, -1, keepdims=True) + EPSILON)
    normal = centered * scale_inv
    return (normal * gain_row + bias_row, normal, scale_inv)


def normalize_back(gradient, normal, scale_inv, gain_row):
    scaled = gradient * gain_row
    return scale_inv * (
        scaled
        - jnp.mean(scaled, -1, keepdims=True)
        - normal * jnp.mean(scaled * normal, -1, keepdims=True)
    )


def gelu_exact(values_in):
    return jax.nn.gelu(values_in, approximate=False)


def gelu_back(pre_act, gradient):
    unused, pullback = jax.vjp(gelu_exact, pre_act)
    return pullback(gradient)[0]


def self_mask(lengths, target, prefix_len):
    rows_pos = jnp.arange(target)[:, None]
    keys_pos = jnp.arange(prefix_len + target)[None, :] - prefix_len
    causal = (keys_pos <= rows_pos)[None]
    inside = keys_pos[None] < lengths[:, None, None]
    return ((keys_pos[None] < 0) | causal & inside)[:, None]


def self_scores(queries, keys_all, allowed, score_scale):
    scores = (
        jnp.einsum("sqhe,skhe->shqk", queries, keys_all, preferred_element_type=jnp.float32)
        * score_scale
    )
    return jnp.where(allowed, scores, NEGATIVE)


def adam_update(gradient, first_moment, second_moment, weight, step_rate):
    first_new = 0.9 * first_moment + 0.1 * gradient
    second_new = 0.999 * second_moment + 0.001 * gradient * gradient
    corrected_one = first_new / (1.0 - 0.9**STEP)
    corrected_two = second_new / (1.0 - 0.999**STEP)
    weight_new = weight - step_rate * (
        corrected_one / (jnp.sqrt(corrected_two) + 1e-08) + 0.01 * weight
    )
    return (first_new, second_new, weight_new)


def local(
    dec_input,
    memory,
    out_grad,
    tgt_lengths,
    src_lengths,
    self_qkv,
    self_out,
    cross_qkv,
    cross_out,
    ffn_in,
    ffn_out,
    norm_gains,
    norm_biases,
    down_w,
    up_w,
    prefix_w,
    down_m,
    down_v,
    up_m,
    up_v,
    prefix_m,
    prefix_v,
    down_outer,
    up_outer,
    prefix_outer,
    down_mom,
    up_mom,
    prefix_mom,
):
    seq_count, target, model_width = dec_input.shape[1:]
    source = memory.shape[2]
    num_heads = HEADS
    head_dim = HDIM
    prefix_len = prefix_w.shape[2]
    total_rows = seq_count * target
    score_scale = head_dim ** (-0.5)
    shard_index = lax.axis_index("mem")
    gathered_down, gathered_up, gathered_prefix = (
        lax.all_gather(down_w[0].astype(jnp.bfloat16), "mem", axis=0, tiled=True),
        lax.all_gather(up_w[0].astype(jnp.bfloat16), "mem", axis=0, tiled=True),
        lax.all_gather(prefix_w[0].astype(jnp.bfloat16), "mem", axis=2, tiled=True),
    )
    tokens = dec_input[0].reshape(total_rows, model_width)
    projected = jnp.einsum(
        "rd,cde->cre", tokens, self_qkv, preferred_element_type=jnp.float32
    ).astype(jnp.bfloat16)
    shaped = projected.reshape(3, seq_count, target, num_heads, head_dim)
    queries = shaped[0]
    prefix_pair = jnp.broadcast_to(
        gathered_prefix.reshape(2, 1, prefix_len, num_heads, head_dim),
        (2, seq_count, prefix_len, num_heads, head_dim),
    )
    keys_all = jnp.concatenate([prefix_pair[0], shaped[1]], axis=1)
    values_all = jnp.concatenate([prefix_pair[1], shaped[2]], axis=1)
    allowed = self_mask(tgt_lengths[0], target, prefix_len)
    masked_self = self_scores(queries, keys_all, allowed, score_scale)
    row_max = jnp.max(masked_self, -1, keepdims=True)
    self_exp = jnp.exp(masked_self - row_max)
    self_total = jnp.sum(self_exp, -1, keepdims=True)
    probs_self = self_exp / self_total
    log_total = row_max + jnp.log(self_total)
    context = (
        jnp.einsum(
            "shqk,skhe->sqhe",
            probs_self.astype(jnp.bfloat16),
            values_all,
            preferred_element_type=jnp.float32,
        )
        .astype(jnp.bfloat16)
        .reshape(total_rows, model_width)
    )
    attended = jnp.dot(context, self_out, preferred_element_type=jnp.float32)
    hidden_one, normal_one, inverse_one = normalize(
        tokens.astype(jnp.float32) + attended, norm_gains[0], norm_biases[0]
    )
    cross_queries = (
        jnp.dot(hidden_one.astype(jnp.bfloat16), cross_qkv[0], preferred_element_type=jnp.float32)
        .astype(jnp.bfloat16)
        .reshape(seq_count, target, num_heads, head_dim)
    )
    mem_rows = memory[0].reshape(seq_count * source, model_width)
    mem_proj = (
        jnp.einsum("rd,cde->cre", mem_rows, cross_qkv[1:], preferred_element_type=jnp.float32)
        .astype(jnp.bfloat16)
        .reshape(2, seq_count, source, num_heads, head_dim)
    )
    positions = shard_index * source + jnp.arange(source)
    valid_keys = (positions[None, :] < src_lengths[0][:, None])[:, None, None, :]
    raw_scores = (
        jnp.einsum(
            "sqhe,skhe->shqk", cross_queries, mem_proj[0], preferred_element_type=jnp.float32
        )
        * score_scale
    )
    masked = jnp.where(valid_keys, raw_scores, NEGATIVE)
    local_max = jnp.max(masked, -1)
    exponent = jnp.exp(masked - local_max[..., None]) * valid_keys.astype(jnp.float32)
    exponent_low = exponent.astype(jnp.bfloat16)
    local_sum = jnp.sum(exponent_low.astype(jnp.float32), -1)
    numerator = jnp.einsum(
        "shqk,skhe->shqe", exponent_low, mem_proj[1], preferred_element_type=jnp.float32
    )
    top_max = lax.pmax(local_max.astype(jnp.bfloat16), "mem").astype(local_max.dtype)
    factor = jnp.exp(local_max - top_max)
    total_sum, numer_sum = (
        lax.psum((factor * local_sum).astype(jnp.bfloat16), "mem").astype(jnp.float32),
        lax.psum((factor[..., None] * numerator).astype(jnp.bfloat16), "mem").astype(jnp.float32),
    )
    cross_ctx = numer_sum / total_sum[..., None]
    cross_low = (
        cross_ctx.transpose(0, 2, 1, 3).reshape(total_rows, model_width).astype(jnp.bfloat16)
    )
    crossed = jnp.dot(cross_low, cross_out, preferred_element_type=jnp.float32)
    hidden_two, normal_two, inverse_two = normalize(
        hidden_one + crossed, norm_gains[1], norm_biases[1]
    )
    normed = hidden_two.astype(jnp.bfloat16)
    ffn_pre = jnp.dot(normed, ffn_in, preferred_element_type=jnp.float32)
    ffn_act = gelu_exact(ffn_pre).astype(jnp.bfloat16)
    ffn_result = jnp.dot(ffn_act, ffn_out, preferred_element_type=jnp.float32)
    adapt_pre = jnp.dot(normed, gathered_down, preferred_element_type=jnp.float32)
    adapt_act = gelu_exact(adapt_pre).astype(jnp.bfloat16)
    adapted = jnp.dot(adapt_act, gathered_up, preferred_element_type=jnp.float32)
    output_rows, normal_three, inverse_three = normalize(
        hidden_two + ffn_result + ADAPTER_SCALE * adapted, norm_gains[2], norm_biases[2]
    )
    live_rows = (
        (jnp.arange(target)[None, :] < tgt_lengths[0][:, None])
        .astype(jnp.float32)
        .reshape(total_rows, 1)
    )
    grad_three = normalize_back(
        out_grad[0].reshape(total_rows, model_width).astype(jnp.float32) * live_rows,
        normal_three,
        inverse_three,
        norm_gains[2],
    )
    grad_adapted = (ADAPTER_SCALE * grad_three).astype(jnp.bfloat16)
    grad_ffn = grad_three.astype(jnp.bfloat16)
    up_share = up_w.shape[1]
    act_share = lax.dynamic_slice_in_dim(adapt_act, shard_index * up_share, up_share, 1)
    grad_up = jnp.dot(act_share.T, grad_adapted, preferred_element_type=jnp.float32)
    grad_adapt_pre = gelu_back(
        adapt_pre, jnp.dot(grad_adapted, gathered_up.T, preferred_element_type=jnp.float32)
    ).astype(jnp.bfloat16)
    down_share = down_w.shape[1]
    normed_share = lax.dynamic_slice_in_dim(normed, shard_index * down_share, down_share, 1)
    grad_down = jnp.dot(normed_share.T, grad_adapt_pre, preferred_element_type=jnp.float32)
    grad_ffn_pre = gelu_back(
        ffn_pre, jnp.dot(grad_ffn, ffn_out.T, preferred_element_type=jnp.float32)
    ).astype(jnp.bfloat16)
    grad_hidden_two = (
        grad_three
        + jnp.dot(grad_ffn_pre, ffn_in.T, preferred_element_type=jnp.float32)
        + jnp.dot(grad_adapt_pre, gathered_down.T, preferred_element_type=jnp.float32)
    )
    grad_two = normalize_back(grad_hidden_two, normal_two, inverse_two, norm_gains[1])
    grad_cross = (
        jnp.dot(grad_two.astype(jnp.bfloat16), cross_out.T, preferred_element_type=jnp.float32)
        .astype(jnp.bfloat16)
        .reshape(seq_count, target, num_heads, head_dim)
        .transpose(0, 2, 1, 3)
    )
    weight_scale = factor / total_sum
    grad_probs = jnp.einsum(
        "shqe,skhe->shqk", grad_cross, mem_proj[1], preferred_element_type=jnp.float32
    )
    cross_delta = jnp.sum(grad_cross.astype(jnp.float32) * cross_ctx, -1)
    grad_scores = (
        exponent * weight_scale[..., None] * (grad_probs - cross_delta[..., None])
    ).astype(jnp.bfloat16)
    query_part = (
        jnp.einsum("shqk,skhe->sqhe", grad_scores, mem_proj[0], preferred_element_type=jnp.float32)
        * score_scale
    ).reshape(total_rows, model_width)
    grad_mem_keys = (
        jnp.einsum(
            "shqk,sqhe->skhe", grad_scores, cross_queries, preferred_element_type=jnp.float32
        )
        * score_scale
    ).astype(jnp.bfloat16)
    grad_mem_values = jnp.einsum(
        "shqk,shqe->skhe",
        exponent_low.astype(jnp.float32),
        grad_cross.astype(jnp.float32) * weight_scale[..., None],
        precision=lax.Precision.HIGHEST,
    ).astype(jnp.bfloat16)
    grad_mem_pair = jnp.stack([grad_mem_keys, grad_mem_values]).reshape(
        2, seq_count * source, model_width
    )
    grad_memory = jnp.einsum(
        "cre,cde->rd", grad_mem_pair, cross_qkv[1:], preferred_element_type=jnp.float32
    )
    grad_queries = lax.psum(query_part.astype(jnp.bfloat16), "mem")
    from_queries = jnp.dot(grad_queries, cross_qkv[0].T, preferred_element_type=jnp.float32)
    grad_one = normalize_back(grad_two + from_queries, normal_one, inverse_one, norm_gains[0])
    grad_context = (
        jnp.dot(grad_one.astype(jnp.bfloat16), self_out.T, preferred_element_type=jnp.float32)
        .astype(jnp.bfloat16)
        .reshape(seq_count, target, num_heads, head_dim)
    )
    probs_again = jnp.exp(self_scores(queries, keys_all, allowed, score_scale) - log_total)
    grad_weights = jnp.einsum(
        "sqhe,skhe->shqk", grad_context, values_all, preferred_element_type=jnp.float32
    )
    self_delta = jnp.sum(probs_again * grad_weights, -1, keepdims=True)
    grad_self_scores = (probs_again * (grad_weights - self_delta)).astype(jnp.bfloat16)
    grad_queries_self = (
        jnp.einsum(
            "shqk,skhe->sqhe", grad_self_scores, keys_all, preferred_element_type=jnp.float32
        )
        * score_scale
    ).astype(jnp.bfloat16)
    grad_keys_all = (
        jnp.einsum("shqk,sqhe->skhe", grad_self_scores, queries, preferred_element_type=jnp.float32)
        * score_scale
    )
    grad_values_all = jnp.einsum(
        "shqk,sqhe->skhe",
        probs_again.astype(jnp.bfloat16),
        grad_context,
        preferred_element_type=jnp.float32,
    )
    grad_prefix_full = jnp.stack(
        [jnp.sum(grad_keys_all[:, :prefix_len], 0), jnp.sum(grad_values_all[:, :prefix_len], 0)]
    ).reshape(2, prefix_len, model_width)
    grad_new = jnp.stack(
        [
            grad_queries_self,
            grad_keys_all[:, prefix_len:].astype(jnp.bfloat16),
            grad_values_all[:, prefix_len:].astype(jnp.bfloat16),
        ]
    ).reshape(3, total_rows, model_width)
    grad_tokens = grad_one + jnp.einsum(
        "cre,cde->rd", grad_new, self_qkv, preferred_element_type=jnp.float32
    )
    prefix_share = prefix_w.shape[3]
    grad_prefix = lax.dynamic_slice_in_dim(
        grad_prefix_full, shard_index * prefix_share, prefix_share, 2
    )
    new_down_m, new_down_v, new_down_w = adam_update(grad_down[None], down_m, down_v, down_w, 0.06)
    new_up_m, new_up_v, new_up_w = adam_update(grad_up[None], up_m, up_v, up_w, 0.02)
    new_prefix_m, new_prefix_v, new_prefix_w = adam_update(
        grad_prefix[None], prefix_m, prefix_v, prefix_w, 2.0
    )
    summed = (
        lax.psum((down_outer - new_down_w[0]).astype(jnp.bfloat16), "grp").astype(jnp.float32),
        lax.psum((up_outer - new_up_w[0]).astype(jnp.bfloat16), "grp").astype(jnp.float32),
        lax.psum((prefix_outer - new_prefix_w[0]).astype(jnp.bfloat16), "grp").astype(jnp.float32),
    )
    group_count = lax.axis_size("grp")
    outer_results = []
    for outer_weight, momentum, difference in (
        (down_outer, down_mom, summed[0]),
        (up_outer, up_mom, summed[1]),
        (prefix_outer, prefix_mom, summed[2]),
    ):
        average = difference / group_count
        momentum_new = OUTER_MOMENTUM * momentum + average
        outer_results.append(momentum_new)
        outer_results.append(outer_weight - OUTER_RATE * (average + OUTER_MOMENTUM * momentum_new))
    return (
        output_rows.astype(jnp.bfloat16).reshape(1, seq_count, target, model_width),
        grad_tokens.reshape(1, seq_count, target, model_width),
        grad_memory.reshape(1, seq_count, source, model_width),
        grad_down[None],
        grad_up[None],
        grad_prefix[None],
        new_down_m,
        new_down_v,
        new_down_w,
        new_up_m,
        new_up_v,
        new_up_w,
        new_prefix_m,
        new_prefix_v,
        new_prefix_w,
        outer_results[0],
        outer_results[1],
        outer_results[2],
        outer_results[3],
        outer_results[4],
        outer_results[5],
    )


def solution(mesh):
    placed = (
        P("grp", None, None, None),
        P("grp", None, "mem", None),
        P("grp", None, None, None),
        P("grp", None),
        P("grp", None),
        P(),
        P(),
        P(),
        P(),
        P(),
        P(),
        P(),
        P(),
        P("grp", "mem", None),
        P("grp", "mem", None),
        P("grp", None, None, "mem"),
        P("grp", "mem", None),
        P("grp", "mem", None),
        P("grp", "mem", None),
        P("grp", "mem", None),
        P("grp", None, None, "mem"),
        P("grp", None, None, "mem"),
        P("mem", None),
        P("mem", None),
        P(None, None, "mem"),
        P("mem", None),
        P("mem", None),
        P(None, None, "mem"),
    )
    return jax.shard_map(
        local,
        mesh=mesh,
        in_specs=placed,
        out_specs=(
            P("grp", None, None, None),
            P("grp", None, None, None),
            P("grp", None, "mem", None),
            P("grp", "mem", None),
            P("grp", "mem", None),
            P("grp", None, None, "mem"),
            P("grp", "mem", None),
            P("grp", "mem", None),
            P("grp", "mem", None),
            P("grp", "mem", None),
            P("grp", "mem", None),
            P("grp", "mem", None),
            P("grp", None, None, "mem"),
            P("grp", None, None, "mem"),
            P("grp", None, None, "mem"),
            P("mem", None),
            P("mem", None),
            P("mem", None),
            P("mem", None),
            P(None, None, "mem"),
            P(None, None, "mem"),
        ),
        check_vma=False,
    )
```

profile of v0, /device:TPU:0, one launch (start us, length us, event | category | flops | bytes accessed | tf_op | source)
XLA Modules:
  0.0 756.5 jit_solution(6779724929877018771)
XLA Ops:
  11.7 22.9 %all-gather = bf16[1,2,30,1024]{3,1,2,0:T(2,128)(2,1)S(1)} all-gather(bf16[1,2,30,128]{3,1,2,0:T(2,128)(2,1)S(1)} %convert_element_type.209), channel_id=2, replica_groups=mesh['grp'=4,'mem'=8] {'mem'}, dimensions={3}, use_global_device_ids=true | all-gather | bytes 138240 | tf_op jit(solution)/shard_map/all_gather | solution.py:111
  49.0 10.2 %convert_bitcast_fusion = bf16[3,1024,1024]{1,2,0:T(8,128)(2,1)S(1)} fusion(bf16[3,1024,1024]{2,1,0:T(8,128)(2,1)} %param.33, bf16[1024,1024,1]{1,0,2:T(8,128)(2,1)} %bitcast.257), kind=kOutput, calls=%fused_computation.39 | convolution fusion | flops 6445596672 | bytes 14680064 | tf_op jit(solution)/shard_map/rd,cde->cre/dot_general | solution.py:114
  62.1 4.5 squeeze.35
  69.9 4.5 squeeze.36
  74.4 4.5 squeeze.37
  81.6 9.4 %fusion.15 = (f32[4,16,256]{2,1,0:T(8,128)S(1)}, f32[4,16,256,286]{2,3,1,0:T(8,128)}) fusion(pred[4,256,286]{1,2,0:T(8,128)(4,1)S(1)} %and_or_fusion, bf16[4,256,16,64]{1,3,2,0:T(8,128)(2,1)S(1)} %copy.107, bf16[4,30,16,64]{1,3,2,0:T(8,128)(2,1)S(1)} %broadcast_in_dim.46, bf16[4,256,16,64]{1,0,3,2:T(4,128)(2,1)S(1)} %copy-done.7), kind=kOutput, calls=%fused_computation.31 | convolution fusion | flops 618512384 | bytes 23541760 | tf_op jit(solution)/shard_map/sqhe,skhe->shqk/dot_general | solution.py:53
  91.1 12.1 %fusion.6 = f32[4,16,256]{2,1,0:T(8,128)} fusion(f32[4,16,256]{2,1,0:T(8,128)S(1)} %get-tuple-element.71, f32[4,16,256,286]{2,3,1,0:T(8,128)} %get-tuple-element.72, pred[4,256,286]{1,2,0:T(8,128)(4,1)S(1)} %and_or_fusion), kind=kLoop, calls=%fused_computation.23 | loop fusion | flops 18726912 | bytes 19167232 | tf_op jit(solution)/shard_map/reduce_sum | solution.py:129
  104.5 12.5 %convert_bitcast_fusion.1 = bf16[4,256,16,64]{1,3,2,0:T(8,128)(2,1)S(1)} fusion(f32[4,16,256]{2,1,0:T(8,128)} %fusion.6, f32[4,16,256]{2,1,0:T(8,128)S(1)} %get-tuple-element.71, f32[4,16,256,286]{2,3,1,0:T(8,128)} %get-tuple-element.72, pred[4,256,286]{1,2,0:T(8,128)(4,1)S(1)} %and_or_fusion, bf16[4,256,16,64]{1,3,2,0:T(8,128)(2,1)} %copy.105, ...), kind=kOutput, calls=%fused_computation.131 | convolution fusion | flops 628948992 | bytes 23607296 | tf_op jit(solution)/shard_map/shqk,skhe->sqhe/dot_general | solution.py:133
  124.0 5.3 fusion.80
  129.3 6.3 reshape.385
  135.7 5.8 copy.112
  141.6 4.7 fusion.30
  146.3 33.8 %pmax.7 = bf16[4,16,256]{2,1,0:T(8,128)(2,1)} all-reduce(bf16[4,16,256]{2,1,0:T(8,128)(2,1)S(1)} %convert_element_type.220), channel_id=1, replica_groups=mesh['grp'=4,'mem'=8] {'mem'}, use_global_device_ids=true, to_apply=%region_5.6 | all-reduce | flops 16384 | bytes 65536 | tf_op jit(solution)/shard_map/pmax | solution.py:173
  190.5 35.4 %psum.43 = bf16[4,16,256]{2,1,0:T(8,128)(2,1)S(1)} all-reduce(bf16[4,16,256]{2,1,0:T(8,128)(2,1)} %get-tuple-element.48), channel_id=1, replica_groups=mesh['grp'=4,'mem'=8] {'mem'}, use_global_device_ids=true, to_apply=%region_8.9 | all-reduce | flops 16384 | bytes 65536 | tf_op jit(solution)/shard_map/psum | solution.py:176
  230.1 56.9 %all-reduce.5.cloned.1.call-done = bf16[4,16,256,64]{2,3,1,0:T(8,128)(2,1)} async-done(((bf16[4,16,256,64]{2,3,1,0:T(8,128)(2,1)}), bf16[4,16,256,64]{2,3,1,0:T(8,128)(2,1)}) %all-reduce.5.cloned.1.call-update) | async-done | bytes 2097168 | tf_op jit(solution)/shard_map/psum | solution.py:177
  296.7 43.9 %fusion = (f32[1024,4096]{1,0:T(8,128)}, f32[1024,4096]{1,0:T(8,128)}) fusion(bf16[1024,1024]{1,0:T(8,128)(2,1)S(1)} %fusion.31, bf16[1024,4096]{1,0:T(8,128)(2,1)S(1)} %bitcast.256), kind=kOutput, calls=%fused_computation.7 | convolution fusion | flops 8849981440 | bytes 44040192 | tf_op jit(solution)/shard_map/dot_general | solution.py:188
  340.6 19.3 %fusion.12 = f32[1024,1024]{1,0:T(8,128)} fusion(bf16[4096,1024]{1,0:T(8,128)(2,1)} %param.38, f32[1024,4096]{1,0:T(8,128)} %get-tuple-element.79, f32[1024,4096]{1,0:T(8,128)} %get-tuple-element.80), kind=kOutput, calls=%fused_computation.28 | convolution fusion | flops 8602517504 | bytes 46137344 | tf_op jit(solution)/shard_map/dot_general | solution.py:190
  359.8 8.6 %multiply_convert_fusion.9 = (bf16[1024,512]{0,1:T(8,128)(2,1)S(1)}, f32[1024,512]{0,1:T(8,128)}, f32[1024,512]{0,1:T(8,128)}) fusion(bf16[1024,1024]{1,0:T(8,128)(2,1)} %copy-done.27, bf16[1,1024,512]{2,1,0:T(8,128)(2,1)} %all-gather.6.cloned.1.call-done), kind=kOutput, calls=%fused_computation.114 | convolution fusion | flops 1107820544 | bytes 8388608 | tf_op jit(solution)/shard_map/dot_general | solution.py:191
  371.2 4.9 fusion.163
  383.2 28.4 %fusion.14 = f32[1024,1024]{1,0:T(8,128)} fusion(bf16[1024,4096]{1,0:T(8,128)(2,1)} %param.37, f32[1024,4096]{1,0:T(8,128)} %get-tuple-element.79, f32[1024,4096]{1,0:T(8,128)} %get-tuple-element.80, bf16[4096,1024]{1,0:T(8,128)(2,1)} %param.38, f32[1024,1024]{1,0:T(8,128)} %get-tuple-element.57), kind=kOutput, calls=%fused_computation.30 | convolution fusion | flops 17239638016 | bytes 58720256 | tf_op jit(solution)/shard_map/dot_general | solution.py:224
  411.6 5.7 add_convert_fusion.3
  419.0 4.2 fusion.145
  425.2 4.2 fusion.74
  429.4 6.4 reshape.381
  435.8 6.0 copy.119
  444.7 4.2 fusion.113
  452.6 3.7 multiply_convert_fusion.5
  468.4 5.4 fusion.91
  478.7 4.6 fusion.94
  486.9 99.4 %all-reduce.7.cloned.1.call-done = bf16[1024,1024]{0,1:T(8,128)(2,1)} async-done(((bf16[1024,1024]{0,1:T(8,128)(2,1)}), bf16[1024,1024]{0,1:T(8,128)(2,1)}) %all-reduce.7.cloned.1.call-update) | async-done | bytes 2097168 | tf_op jit(solution)/shard_map/psum | solution.py:264
  586.3 9.3 %fusion.144 = (f32[1024]{0:T(1024)S(1)}, f32[1024]{0:T(1024)S(1)}, f32[1024,1024]{1,0:T(8,128)S(1)}) fusion(f32[1024]{0:T(1024)S(1)} %copy-done.64, f32[1024,1024]{1,0:T(8,128)} %copy-done.20, f32[1024]{0:T(1024)S(1)} %copy-done.57, f32[1024]{0:T(1024)S(1)} %bitcast.249, bf16[1024,1024]{0,1:T(8,128)(2,1)} %all-reduce.7.cloned.1.call-done, ...), kind=kOutput, calls=%fused_computation.237 | convolution fusion | flops 2161113088 | bytes 21008384 | tf_op jit(solution)/shard_map/dot_general | solution.py:265
  597.7 4.2 fusion.77
  601.9 6.3 reshape.386
  608.2 6.0 copy.124
  614.3 13.8 %fusion.34 = f32[4,286,16,64]{1,3,2,0:T(8,128)} fusion(bf16[4,256,16,64]{1,3,2,0:T(8,128)(2,1)} %copy.124, f32[4,16,256]{2,1,0:T(8,128)S(1)} %log_add_fusion, f32[4,16,256,286]{2,3,1,0:T(8,128)} %get-tuple-element.72, pred[4,256,286]{1,2,0:T(8,128)(4,1)S(1)} %copy-done.15), kind=kOutput, calls=%fused_computation.90 | convolution fusion | flops 618528768 | bytes 25884672 | tf_op jit(solution)/shard_map/shqk,sqhe->skhe/dot_general | solution.py:288
  630.8 5.0 slice.125
  635.8 17.1 %multiply_reduce_fusion = (f32[4,16,256]{2,1,0:T(8,128)}, f32[4,16,256,286]{2,3,1,0:T(8,128)}) fusion(f32[4,16,256]{2,1,0:T(8,128)S(1)} %log_add_fusion, f32[4,16,256,286]{2,3,1,0:T(8,128)} %get-tuple-element.72, pred[4,256,286]{1,2,0:T(8,128)(4,1)S(1)} %copy-done.15, bf16[4,256,16,64]{1,3,2,0:T(8,128)(2,1)} %copy.124, bf16[4,256,16,64]{1,3,2,0:T(8,128)(2,1)} %copy.105, ...), kind=kOutput, calls=%fused_computation.2 | convolution fusion | flops 627884032 | bytes 42350592 | tf_op jit(solution)/shard_map/sqhe,skhe->shqk/dot_general | solution.py:273
  652.9 14.7 %multiply_convert_fusion = bf16[4,16,256,286]{2,3,1,0:T(8,128)(2,1)S(1)} fusion(f32[4,16,256,286]{2,3,1,0:T(8,128)} %get-tuple-element.87, f32[4,16,256]{2,1,0:T(8,128)} %get-tuple-element.86, f32[4,16,256]{2,1,0:T(8,128)S(1)} %log_add_fusion, f32[4,16,256,286]{2,3,1,0:T(8,128)} %get-tuple-element.72, pred[4,256,286]{1,2,0:T(8,128)(4,1)S(1)} %copy-done.15), kind=kLoop, calls=%fused_computation.1 | loop fusion | flops 28114944 | bytes 47282176 | tf_op jit(solution)/shard_map/convert_element_type | solution.py:277
  671.3 5.6 multiply_bitcast_fusion
  678.9 5.0 slice.126
  684.1 6.2 copy.148
  690.3 6.6 reshape.384
  697.9 11.0 %psum.47 = bf16[2,30,128]{2,0,1:T(2,128)(2,1)S(1)} all-reduce(bf16[2,30,128]{2,0,1:T(2,128)(2,1)S(1)} %get-tuple-element.29), channel_id=1, replica_groups=mesh['grp'=4,'mem'=8] {'grp'}, use_global_device_ids=true, to_apply=%region_26.27 | all-reduce | flops 7680 | bytes 30720 | tf_op jit(solution)/shard_map/psum | solution.py:319
  708.9 6.2 copy.147
  715.1 6.5 reshape.383
  721.6 6.2 copy.146
  727.7 6.5 reshape.382
  734.9 14.7 %bitcast_add_fusion = f32[1024,1024]{1,0:T(8,128)} fusion(bf16[3,1024,1024]{2,1,0:T(8,128)(2,1)} %param.33, bf16[1,1024,1024]{2,1,0:T(8,128)(2,1)} %reshape.384, bf16[1,1024,1024]{2,1,0:T(8,128)(2,1)} %reshape.383, bf16[1,1024,1024]{2,1,0:T(8,128)(2,1)} %reshape.382, f32[1024]{0:T(1024)S(1)} %broadcast_multiply_fusion, f32[1024,1024]{1,0:T(8,128)} %copy-done.20, ...), kind=kOutput, calls=%fused_computation.48 | convolution fusion | flops 6456082432 | bytes 25182208 | tf_op jit(solution)/shard_map/cre,cde->rd/dot_general | solution.py:304
  (250 shorter events, 112.5 us)
Async XLA Ops:
  7.2 284.4 %copy-start = (bf16[1024,1024]{1,0:T(8,128)(2,1)S(1)}, bf16[1024,1024]{1,0:T(8,128)(2,1)}, u32[]{:S(2)}) copy-start(bf16[1024,1024]{1,0:T(8,128)(2,1)} %param.36) | copy-start | bytes 6291460
  7.2 279.8 %all-reduce.5.cloned.1.call-start = ((), (), s32[]{:S(2)}) async-start(), calls=%async_computation | async-start | bytes 4194304 | tf_op jit(solution)/shard_map/psum | solution.py:177
  9.5 113.1 %copy-start.65 = (f32[1,1024]{1,0:T(1,128)}, f32[1,1024]{1,0:T(1,128)S(1)}, u32[]{:S(2)}) copy-start(f32[1,1024]{1,0:T(1,128)S(1)} %get-tuple-element.64) | copy-start | bytes 12292
  9.5 217.6 %copy-start.48 = (f32[1,1024]{1,0:T(1,128)}, f32[1,1024]{1,0:T(1,128)S(1)}, u32[]{:S(2)}) copy-start(f32[1,1024]{1,0:T(1,128)S(1)} %get-tuple-element.63) | copy-start | bytes 12292
  43.5 98.0 %copy-start.9 = (bf16[4,64,16,64]{1,0,3,2:T(4,128)(2,1)}, bf16[4,64,16,64]{1,0,3,2:T(4,128)(2,1)S(1)}, u32[]{:S(2)}) copy-start(bf16[4,64,16,64]{1,0,3,2:T(4,128)(2,1)S(1)} %squeeze.39) | copy-start | bytes 1572868
  81.0 10.0 %copy-start.11 = (bf16[4,256,16,64]{1,3,2,0:T(8,128)(2,1)}, bf16[4,256,16,64]{1,3,2,0:T(8,128)(2,1)S(1)}, u32[]{:S(2)}) copy-start(bf16[4,256,16,64]{1,3,2,0:T(8,128)(2,1)S(1)} %copy.107) | copy-start | bytes 6291460
  81.3 23.1 %copy-start.14 = (pred[4,256,286]{1,2,0:T(8,128)(4,1)}, pred[4,256,286]{1,2,0:T(8,128)(4,1)S(1)}, u32[]{:S(2)}) copy-start(pred[4,256,286]{1,2,0:T(8,128)(4,1)S(1)} %and_or_fusion) | copy-start | bytes 878596
  81.6 9.5 %copy-start.16 = (bf16[4,30,16,64]{1,3,2,0:T(8,128)(2,1)}, bf16[4,30,16,64]{1,3,2,0:T(8,128)(2,1)S(1)}, u32[]{:S(2)}) copy-start(bf16[4,30,16,64]{1,3,2,0:T(8,128)(2,1)S(1)} %broadcast_in_dim.46) | copy-start | bytes 737284
  91.1 13.4 %copy-start.39 = (f32[4,16,256]{2,1,0:T(8,128)}, f32[4,16,256]{2,1,0:T(8,128)S(1)}, u32[]{:S(2)}) copy-start(f32[4,16,256]{2,1,0:T(8,128)S(1)} %get-tuple-element.71) | copy-start | bytes 196612
  104.5 12.5 %copy-start.18 = (bf16[4,30,16,64]{1,3,2,0:T(8,128)(2,1)}, bf16[4,30,16,64]{1,3,2,0:T(8,128)(2,1)S(1)}, u32[]{:S(2)}) copy-start(bf16[4,30,16,64]{1,3,2,0:T(8,128)(2,1)S(1)} %broadcast_in_dim.43) | copy-start | bytes 737284
  122.0 169.6 %copy-start.56 = (f32[1024]{0:T(1024)}, f32[1024]{0:T(1024)S(1)}, u32[]{:S(2)}) copy-start(f32[1024]{0:T(1024)S(1)} %broadcast_multiply_fusion.7) | copy-start | bytes 12292
  122.6 6.7 copy-start.62
  141.6 38.5 %copy-start.58 = (f32[4,64]{1,0:T(4,128)}, f32[4,64]{1,0:T(4,128)S(1)}, u32[]{:S(2)}) copy-start(f32[4,64]{1,0:T(4,128)S(1)} %get-tuple-element.52) | copy-start | bytes 3076
  141.6 38.5 %copy-start.60 = (pred[4,64]{1,0:T(4,128)(4,1)}, pred[4,64]{1,0:T(4,128)(4,1)S(1)}, u32[]{:S(2)}) copy-start(pred[4,64]{1,0:T(4,128)(4,1)S(1)} %get-tuple-element.53) | copy-start | bytes 772
  146.3 40.9 %copy-start.30 = (f32[4,16,256]{2,1,0:T(8,128)}, f32[4,16,256]{2,1,0:T(8,128)S(1)}, u32[]{:S(2)}) copy-start(f32[4,16,256]{2,1,0:T(8,128)S(1)} %get-tuple-element.75) | copy-start | bytes 196612
  146.3 38.8 %copy-start.23 = (bf16[4,64,16,64]{3,1,2,0:T(8,128)(2,1)S(1)}, bf16[4,64,16,64]{3,1,2,0:T(8,128)(2,1)}, u32[]{:S(2)}) copy-start(bf16[4,64,16,64]{3,1,2,0:T(8,128)(2,1)} %copy.120) | copy-start | bytes 1572868
  187.3 172.6 %all-gather.6.cloned.1.call-start = ((), (), s32[]{:S(2)}) async-start(), calls=%async_computation.2 | async-start | bytes 1179648 | tf_op jit(solution)/shard_map/all_gather | solution.py:109
  188.0 183.2 %all-gather.8.cloned.1.call-start = ((), (), s32[]{:S(2)}) async-start(), calls=%async_computation.3 | async-start | bytes 1179648 | tf_op jit(solution)/shard_map/all_gather | solution.py:110
  189.7 293.6 %all-reduce.9.cloned.1.call-start = ((), (), s32[]{:S(2)}) async-start(), calls=%async_computation.4 | async-start | bytes 524288 | tf_op jit(solution)/shard_map/psum | solution.py:317
  226.5 64.6 %copy-start.37 = (f32[4,16,256]{2,1,0:T(8,128)}, f32[4,16,256]{2,1,0:T(8,128)S(1)}, u32[]{:S(2)}) copy-start(f32[4,16,256]{2,1,0:T(8,128)S(1)} %convert_element_type.228) | copy-start | bytes 196612
  296.7 43.9 %copy-start.27 = (bf16[1024,1024]{1,0:T(8,128)(2,1)}, bf16[1024,1024]{1,0:T(8,128)(2,1)S(1)}, u32[]{:S(2)}) copy-start(bf16[1024,1024]{1,0:T(8,128)(2,1)S(1)} %fusion.31) | copy-start | bytes 6291460
  368.4 7.7 %copy-start.29 = (bf16[1024,512]{0,1:T(8,128)(2,1)}, bf16[1024,512]{0,1:T(8,128)(2,1)S(1)}, u32[]{:S(2)}) copy-start(bf16[1024,512]{0,1:T(8,128)(2,1)S(1)} %get-tuple-element.46) | copy-start | bytes 3145732
  411.5 6.2 copy-start.3
  411.5 7.4 copy-start.26
  435.8 6.1 copy-start.34
  444.7 7.9 %copy-start.24 = (bf16[4,64,16,64]{3,1,2,0:T(8,128)(2,1)S(1)}, bf16[4,64,16,64]{3,1,2,0:T(8,128)(2,1)}, u32[]{:S(2)}) copy-start(bf16[4,64,16,64]{3,1,2,0:T(8,128)(2,1)} %copy.120) | copy-start | bytes 1572868
  444.7 7.9 %copy-start.31 = (f32[4,16,256]{2,1,0:T(8,128)S(1)}, f32[4,16,256]{2,1,0:T(8,128)}, u32[]{:S(2)}) copy-start(f32[4,16,256]{2,1,0:T(8,128)} %copy-done.30) | copy-start | bytes 196612
  444.7 7.9 %copy-start.44 = (f32[4,16,256]{2,1,0:T(8,128)S(1)}, f32[4,16,256]{2,1,0:T(8,128)}, u32[]{:S(2)}) copy-start(f32[4,16,256]{2,1,0:T(8,128)} %convert_divide_fusion.1) | copy-start | bytes 196612
  444.7 7.9 %copy-start.59 = (f32[4,64]{1,0:T(4,128)S(1)}, f32[4,64]{1,0:T(4,128)}, u32[]{:S(2)}) copy-start(f32[4,64]{1,0:T(4,128)} %copy-done.58) | copy-start | bytes 3076
  444.7 7.9 %copy-start.61 = (pred[4,64]{1,0:T(4,128)(4,1)S(1)}, pred[4,64]{1,0:T(4,128)(4,1)}, u32[]{:S(2)}) copy-start(pred[4,64]{1,0:T(4,128)(4,1)} %copy-done.60) | copy-start | bytes 772
  448.9 137.4 %all-reduce.7.cloned.1.call-start = ((), (), s32[]{:S(2)}) async-start(), calls=%async_computation.1 | async-start | bytes 4194304 | tf_op jit(solution)/shard_map/psum | solution.py:264
  478.6 6.5 copy-start.36
  478.6 6.5 copy-start.43
  478.7 107.7 %copy-start.57 = (f32[1024]{0:T(1024)S(1)}, f32[1024]{0:T(1024)}, u32[]{:S(2)}) copy-start(f32[1024]{0:T(1024)} %copy-done.56) | copy-start | bytes 12292
  478.7 107.7 %copy-start.64 = (f32[1024]{0:T(1024)S(1)}, f32[1024]{0:T(1024)}, u32[]{:S(2)}) copy-start(f32[1024]{0:T(1024)} %copy-done.62) | copy-start | bytes 12292
  478.7 107.7 %copy-start.67 = (f32[1,1024]{1,0:T(1,128)S(1)}, f32[1,1024]{1,0:T(1,128)}, u32[]{:S(2)}) copy-start(f32[1,1024]{1,0:T(1,128)} %copy-done.65) | copy-start | bytes 12292
  586.3 11.4 %copy-start.22 = (f32[1024,1024]{1,0:T(8,128)S(1)}, f32[1024,1024]{1,0:T(8,128)}, u32[]{:S(2)}) copy-start(f32[1024,1024]{1,0:T(8,128)} %copy-done.20) | copy-start | bytes 12582916
  586.3 11.3 %copy-start.74 = (bf16[1024,1024]{1,0:T(8,128)(2,1)S(1)}, bf16[1024,1024]{1,0:T(8,128)(2,1)}, u32[]{:S(2)}) copy-start(bf16[1024,1024]{1,0:T(8,128)(2,1)} %param.34) | copy-start | bytes 6291460
  608.2 6.0 copy-start.15
  628.1 7.7 %copy-start.19 = (bf16[4,30,16,64]{1,3,2,0:T(8,128)(2,1)S(1)}, bf16[4,30,16,64]{1,3,2,0:T(8,128)(2,1)}, u32[]{:S(2)}) copy-start(bf16[4,30,16,64]{1,3,2,0:T(8,128)(2,1)} %copy-done.18) | copy-start | bytes 737284
  652.9 14.7 %copy-start.12 = (bf16[4,256,16,64]{1,3,2,0:T(8,128)(2,1)S(1)}, bf16[4,256,16,64]{1,3,2,0:T(8,128)(2,1)}, u32[]{:S(2)}) copy-start(bf16[4,256,16,64]{1,3,2,0:T(8,128)(2,1)} %copy-done.11) | copy-start | bytes 6291460
  652.9 14.7 %copy-start.17 = (bf16[4,30,16,64]{1,3,2,0:T(8,128)(2,1)S(1)}, bf16[4,30,16,64]{1,3,2,0:T(8,128)(2,1)}, u32[]{:S(2)}) copy-start(bf16[4,30,16,64]{1,3,2,0:T(8,128)(2,1)} %copy-done.16) | copy-start | bytes 737284
  677.0 6.9 copy-start.28
  690.3 6.8 copy-start.46
  690.3 6.8 copy-start.47
  690.3 6.8 copy-start.51
  690.3 6.8 copy-start.52
  727.7 6.5 copy-start.53
  (35 other events, 107.2 us)
Sparse Core Ops, SparseCore 0:
  187.4 99.5 all-reduce.4
  289.7 39.8 all-gather.5
  332.3 38.8 all-gather.7
  449.0 30.8 all-reduce.8
  484.4 101.8 all-reduce.6
where the time goes:
time: 761 us; the launch traced here: 756 us
  matrix products  266 us (35%)
  waiting for transfers between devices  159 us (21%)
  local copies, waits for them, and re-layouts  149 us (20%)
  blocking collectives  103 us (14%)
  other arithmetic  64.2 us (8%)
  between operations  15.2 us (2%)
    psum x1, waiting for transfers between devices, local(): grad_queries = lax.psum(query_part.astype(jnp.bfloat16), 'mem')  99.4 us
    psum x1, waiting for transfers between devices, local(): lax.psum((factor[..., None] * numerator).astype(jnp.bfloat16), 'mem')  56.9 us
    dot_general x1, matrix products, local(): ffn_pre = jnp.dot(normed, ffn_in, preferred_element_type=jnp.float32)  43.9 us
    another operation x6, local copies, waits for them, and re-layouts, local(): jnp.stack([grad_queries_self, grad_keys_all[:, prefix_len:].astype(jnp.bf...  38.1 us
    psum x1, blocking collectives, local(): lax.psum((factor * local_sum).astype(jnp.bfloat16), 'mem')  35.4 us
    pmax x1, blocking collectives, local(): lax.pmax(local_max.astype(jnp.bfloat16), 'mem').astype(local_max.dtype)  33.8 us
    dot_general x1, matrix products, local(): jnp.dot(grad_ffn_pre, ffn_in.T, preferred_element_type=jnp.float32)  28.4 us
    all_gather x1, blocking collectives, local(): lax.all_gather(prefix_w[0].astype(jnp.bfloat16), 'mem', axis=2, tiled=True)  22.9 us
  transfers between devices with their start and end apart: 5, of which 3 were waited for; matrix products, arithmetic and copies ran while one was open for 17% of the time, Pallas kernels for 0%

commit v1 on v0

v1 whole, which is shorter than its diff:
```python
import jax
import jax.numpy as jnp
from jax import lax
from jax.sharding import PartitionSpec as P

HEADS = 16
HDIM = 64
STEP = 10


EPSILON = 1e-05
NEGATIVE = -1e30
ADAPTER_SCALE = 4.0
OUTER_MOMENTUM = 0.9
OUTER_RATE = 0.7


def normalize(values_in, gain_row, bias_row):
    centered = values_in - jnp.mean(values_in, -1, keepdims=True)
    scale_inv = lax.rsqrt(jnp.mean(centered * centered, -1, keepdims=True) + EPSILON)
    normal = centered * scale_inv
    return (normal * gain_row + bias_row, normal, scale_inv)


def normalize_back(gradient, normal, scale_inv, gain_row):
    scaled = gradient * gain_row
    return scale_inv * (
        scaled
        - jnp.mean(scaled, -1, keepdims=True)
        - normal * jnp.mean(scaled * normal, -1, keepdims=True)
    )


def gelu_exact(values_in):
    return jax.nn.gelu(values_in, approximate=False)


def gelu_back(pre_act, gradient):
    unused, pullback = jax.vjp(gelu_exact, pre_act)
    return pullback(gradient)[0]


def self_mask(length, target, prefix_len):
    rows_pos = jnp.arange(target)[:, None]
    keys_pos = jnp.arange(prefix_len + target)[None, :] - prefix_len
    return ((keys_pos < 0) | (keys_pos <= rows_pos) & (keys_pos < length))[None]


def self_scores(queries, keys_all, allowed, score_scale):
    scores = (
        jnp.einsum("qhe,khe->hqk", queries, keys_all, preferred_element_type=jnp.float32)
        * score_scale
    )
    return jnp.where(allowed, scores, NEGATIVE)


def adam_update(gradient, first_moment, second_moment, weight, step_rate):
    first_new = 0.9 * first_moment + 0.1 * gradient
    second_new = 0.999 * second_moment + 0.001 * gradient * gradient
    corrected_one = first_new / (1.0 - 0.9**STEP)
    corrected_two = second_new / (1.0 - 0.999**STEP)
    weight_new = weight - step_rate * (
        corrected_one / (jnp.sqrt(corrected_two) + 1e-08) + 0.01 * weight
    )
    return (first_new, second_new, weight_new)


def local(
    dec_input,
    memory,
    out_grad,
    tgt_lengths,
    src_lengths,
    self_qkv,
    self_out,
    cross_qkv,
    cross_out,
    ffn_in,
    ffn_out,
    norm_gains,
    norm_biases,
    down_w,
    up_w,
    prefix_w,
    down_m,
    down_v,
    up_m,
    up_v,
    prefix_m,
    prefix_v,
    down_outer,
    up_outer,
    prefix_outer,
    down_mom,
    up_mom,
    prefix_mom,
):
    seq_count, target, model_width = dec_input.shape[1:]
    source = memory.shape[2]
    num_heads = HEADS
    head_dim = HDIM
    prefix_len = prefix_w.shape[2]
    mem_size = lax.axis_size("mem")
    grp_size = lax.axis_size("grp")
    replicas = mem_size // seq_count
    score_scale = head_dim ** (-0.5)
    device = lax.axis_index("mem")
    seq = device % seq_count
    replica = device // seq_count

    def swap(values_in, bits):
        return lax.ppermute(values_in, "mem", [(j, j ^ bits) for j in range(mem_size)])

    def pick(values_in, index):
        return lax.dynamic_index_in_dim(values_in, index, 0, keepdims=False)

    def natural(pieces):
        return jnp.take(jnp.stack(pieces), device ^ jnp.arange(len(pieces)), axis=0)

    def plane_gather(values_in):
        half = values_in.shape[0] // 2
        low, high = values_in[:half], values_in[half:]
        low_one, high_two = swap(low, 1), swap(high, 2)
        low_two, high_one = swap(low, 2), swap(high, 1)
        low_three, high_three = swap(low_two, 1), swap(high_one, 2)
        return [
            values_in,
            jnp.concatenate([low_one, high_one]),
            jnp.concatenate([low_two, high_two]),
            jnp.concatenate([low_three, high_three]),
        ]

    def plane_order(pieces):
        return jnp.take(jnp.stack(pieces), seq ^ jnp.arange(seq_count), axis=0)

    mem_send = [pick(memory[0], seq ^ j) for j in range(seq_count)]
    mem_rows = natural(
        [mem_send[0]] + [swap(mem_send[k % seq_count], k) for k in range(1, mem_size)]
    ).reshape(mem_size * source, model_width)
    prefix = prefix_w[0].astype(jnp.bfloat16)
    bits = 1
    while bits < mem_size:
        other = swap(prefix, bits)
        prefix = jnp.where(
            (device & bits) > 0,
            jnp.concatenate([other, prefix], 2),
            jnp.concatenate([prefix, other], 2),
        )
        bits *= 2

    def gather_rows(values_in):
        pieces = [values_in]
        bits = mem_size // 2
        while bits >= seq_count:
            pieces = pieces + [swap(piece, bits) for piece in pieces]
            bits //= 2
        order = [0]
        bits = replicas // 2
        while bits:
            order = order + [o ^ bits for o in order]
            bits //= 2
        planes = [plane_gather(piece) for piece in pieces]
        every = [None] * mem_size
        for o, plane in zip(order, planes):
            for j in range(seq_count):
                every[o * seq_count + j] = plane[j]
        return natural(every).reshape(mem_size * values_in.shape[0], values_in.shape[1])

    gathered_down = gather_rows(down_w[0].astype(jnp.bfloat16))
    gathered_up = gather_rows(up_w[0].astype(jnp.bfloat16))

    tokens = pick(dec_input[0], seq)
    cotangent = pick(out_grad[0], seq)
    tgt_length = tgt_lengths[0, seq]
    src_length = src_lengths[0, seq]
    projected = jnp.einsum(
        "rd,cde->cre", tokens, self_qkv, preferred_element_type=jnp.float32
    ).astype(jnp.bfloat16)
    shaped = projected.reshape(3, target, num_heads, head_dim)
    queries = shaped[0]
    prefix_pair = prefix.reshape(2, prefix_len, num_heads, head_dim)
    keys_all = jnp.concatenate([prefix_pair[0], shaped[1]], axis=0)
    values_all = jnp.concatenate([prefix_pair[1], shaped[2]], axis=0)
    allowed = self_mask(tgt_length, target, prefix_len)
    masked_self = self_scores(queries, keys_all, allowed, score_scale)
    row_max = jnp.max(masked_self, -1, keepdims=True)
    self_exp = jnp.exp(masked_self - row_max)
    self_total = jnp.sum(self_exp, -1, keepdims=True)
    probs_self = self_exp / self_total
    context = (
        jnp.einsum(
            "hqk,khe->qhe",
            probs_self.astype(jnp.bfloat16),
            values_all,
            preferred_element_type=jnp.float32,
        )
        .astype(jnp.bfloat16)
        .reshape(target, model_width)
    )
    attended = jnp.dot(context, self_out, preferred_element_type=jnp.float32)
    hidden_one, normal_one, inverse_one = normalize(
        tokens.astype(jnp.float32) + attended, norm_gains[0], norm_biases[0]
    )
    cross_queries = (
        jnp.dot(hidden_one.astype(jnp.bfloat16), cross_qkv[0], preferred_element_type=jnp.float32)
        .astype(jnp.bfloat16)
        .reshape(target, num_heads, head_dim)
    )
    mem_proj = (
        jnp.einsum("rd,cde->cre", mem_rows, cross_qkv[1:], preferred_element_type=jnp.float32)
        .astype(jnp.bfloat16)
        .reshape(2, mem_size * source, num_heads, head_dim)
    )
    valid_keys = (jnp.arange(mem_size * source) < src_length)[None, None, :]
    raw_scores = (
        jnp.einsum("qhe,khe->hqk", cross_queries, mem_proj[0], preferred_element_type=jnp.float32)
        * score_scale
    )
    masked = jnp.where(valid_keys, raw_scores, NEGATIVE)
    top_max = jnp.max(masked, -1, keepdims=True)
    exponent = jnp.exp(masked - top_max)
    exponent_low = exponent.astype(jnp.bfloat16)
    total_sum = jnp.sum(exponent_low.astype(jnp.float32), -1)
    numerator = jnp.einsum(
        "hqk,khe->hqe", exponent_low, mem_proj[1], preferred_element_type=jnp.float32
    )
    cross_ctx = numerator / total_sum[..., None]
    cross_low = cross_ctx.transpose(1, 0, 2).reshape(target, model_width).astype(jnp.bfloat16)
    crossed = jnp.dot(cross_low, cross_out, preferred_element_type=jnp.float32)
    hidden_two, normal_two, inverse_two = normalize(
        hidden_one + crossed, norm_gains[1], norm_biases[1]
    )
    normed = hidden_two.astype(jnp.bfloat16)
    ffn_pre = jnp.dot(normed, ffn_in, preferred_element_type=jnp.float32)
    ffn_act = gelu_exact(ffn_pre).astype(jnp.bfloat16)
    ffn_result = jnp.dot(ffn_act, ffn_out, preferred_element_type=jnp.float32)
    adapt_pre = jnp.dot(normed, gathered_down, preferred_element_type=jnp.float32)
    adapt_act = gelu_exact(adapt_pre).astype(jnp.bfloat16)
    adapted = jnp.dot(adapt_act, gathered_up, preferred_element_type=jnp.float32)
    output_rows, normal_three, inverse_three = normalize(
        hidden_two + ffn_result + ADAPTER_SCALE * adapted, norm_gains[2], norm_biases[2]
    )
    output = plane_order(plane_gather(output_rows.astype(jnp.bfloat16)))
    live_rows = (jnp.arange(target) < tgt_length).astype(jnp.float32)[:, None]
    grad_three = normalize_back(
        cotangent.astype(jnp.float32) * live_rows, normal_three, inverse_three, norm_gains[2]
    )
    grad_adapted = (ADAPTER_SCALE * grad_three).astype(jnp.bfloat16)
    grad_ffn = grad_three.astype(jnp.bfloat16)
    grad_adapt_pre = gelu_back(
        adapt_pre, jnp.dot(grad_adapted, gathered_up.T, preferred_element_type=jnp.float32)
    ).astype(jnp.bfloat16)

    def owners_sum(left, right):
        columns = left.shape[1] // replicas
        share = lax.dynamic_slice_in_dim(left, replica * columns, columns, 1)
        partial = jnp.dot(share.T, right, preferred_element_type=jnp.float32)
        partial = partial.reshape(seq_count, columns // seq_count, right.shape[1])
        total = pick(partial, seq)
        low = partial.astype(jnp.bfloat16)
        for j in range(1, seq_count):
            total = total + swap(pick(low, seq ^ j), j).astype(jnp.float32)
        return total

    grad_up = owners_sum(adapt_act, grad_adapted)
    grad_down = owners_sum(normed, grad_adapt_pre)
    grad_ffn_pre = gelu_back(
        ffn_pre, jnp.dot(grad_ffn, ffn_out.T, preferred_element_type=jnp.float32)
    ).astype(jnp.bfloat16)
    grad_hidden_two = (
        grad_three
        + jnp.dot(grad_ffn_pre, ffn_in.T, preferred_element_type=jnp.float32)
        + jnp.dot(grad_adapt_pre, gathered_down.T, preferred_element_type=jnp.float32)
    )
    grad_two = normalize_back(grad_hidden_two, normal_two, inverse_two, norm_gains[1])
    grad_cross = (
        jnp.dot(grad_two.astype(jnp.bfloat16), cross_out.T, preferred_element_type=jnp.float32)
        .astype(jnp.bfloat16)
        .reshape(target, num_heads, head_dim)
        .transpose(1, 0, 2)
    )
    grad_probs = jnp.einsum(
        "hqe,khe->hqk", grad_cross, mem_proj[1], preferred_element_type=jnp.float32
    )
    cross_delta = jnp.sum(grad_cross.astype(jnp.float32) * cross_ctx, -1)
    grad_scores = (
        exponent / total_sum[..., None] * (grad_probs - cross_delta[..., None])
    ).astype(jnp.bfloat16)
    grad_queries = (
        (
            jnp.einsum(
                "hqk,khe->qhe", grad_scores, mem_proj[0], preferred_element_type=jnp.float32
            )
            * score_scale
        )
        .reshape(target, model_width)
        .astype(jnp.bfloat16)
    )
    grad_mem_keys = (
        jnp.einsum("hqk,qhe->khe", grad_scores, cross_queries, preferred_element_type=jnp.float32)
        * score_scale
    ).astype(jnp.bfloat16)
    grad_mem_values = jnp.einsum(
        "hqk,hqe->khe",
        exponent_low,
        (grad_cross.astype(jnp.float32) / total_sum[..., None]).astype(jnp.bfloat16),
        preferred_element_type=jnp.float32,
    ).astype(jnp.bfloat16)
    grad_mem_pair = jnp.stack([grad_mem_keys, grad_mem_values]).reshape(
        2, mem_size * source, model_width
    )
    plane_rows = seq_count * source
    grad_mem_share = lax.dynamic_slice_in_dim(grad_mem_pair, replica * plane_rows, plane_rows, 1)
    grad_mem_rows = (
        jnp.einsum("cre,cde->rd", grad_mem_share, cross_qkv[1:], preferred_element_type=jnp.float32)
        .reshape(seq_count, source, model_width)
        .astype(jnp.bfloat16)
    )
    grad_mem_sent = [pick(grad_mem_rows, seq ^ j) for j in range(seq_count)]
    grad_memory = plane_order(
        [grad_mem_sent[0]] + [swap(grad_mem_sent[j], j) for j in range(1, seq_count)]
    ).astype(jnp.float32)
    from_queries = jnp.dot(grad_queries, cross_qkv[0].T, preferred_element_type=jnp.float32)
    grad_one = normalize_back(grad_two + from_queries, normal_one, inverse_one, norm_gains[0])
    grad_context = (
        jnp.dot(grad_one.astype(jnp.bfloat16), self_out.T, preferred_element_type=jnp.float32)
        .astype(jnp.bfloat16)
        .reshape(target, num_heads, head_dim)
    )
    grad_weights = jnp.einsum(
        "qhe,khe->hqk", grad_context, values_all, preferred_element_type=jnp.float32
    )
    self_delta = jnp.sum(probs_self * grad_weights, -1, keepdims=True)
    grad_self_scores = (probs_self * (grad_weights - self_delta)).astype(jnp.bfloat16)
    grad_queries_self = (
        jnp.einsum("hqk,khe->qhe", grad_self_scores, keys_all, preferred_element_type=jnp.float32)
        * score_scale
    ).astype(jnp.bfloat16)
    grad_keys_all = (
        jnp.einsum("hqk,qhe->khe", grad_self_scores, queries, preferred_element_type=jnp.float32)
        * score_scale
    )
    grad_values_all = jnp.einsum(
        "hqk,qhe->khe",
        probs_self.astype(jnp.bfloat16),
        grad_context,
        preferred_element_type=jnp.float32,
    )
    grad_new = jnp.stack(
        [
            grad_queries_self,
            grad_keys_all[prefix_len:].astype(jnp.bfloat16),
            grad_values_all[prefix_len:].astype(jnp.bfloat16),
        ]
    ).reshape(3, target, model_width)
    grad_tokens = grad_one + jnp.einsum(
        "cre,cde->rd", grad_new, self_qkv, preferred_element_type=jnp.float32
    )
    grad_input = plane_order(plane_gather(grad_tokens.astype(jnp.bfloat16))).astype(jnp.float32)
    grad_prefix_full = jnp.stack(
        [grad_keys_all[:prefix_len], grad_values_all[:prefix_len]]
    ).reshape(2, prefix_len, model_width)
    prefix_share = prefix_w.shape[3]
    plane_columns = lax.dynamic_slice_in_dim(
        grad_prefix_full, replica * seq_count * prefix_share, seq_count * prefix_share, 2
    )
    grad_prefix = lax.dynamic_slice_in_dim(plane_columns, seq * prefix_share, prefix_share, 2)
    plane_low = plane_columns.astype(jnp.bfloat16)
    for j in range(1, seq_count):
        grad_prefix = grad_prefix + swap(
            lax.dynamic_slice_in_dim(plane_low, (seq ^ j) * prefix_share, prefix_share, 2), j
        ).astype(jnp.float32)
    new_down_m, new_down_v, new_down_w = adam_update(grad_down[None], down_m, down_v, down_w, 0.06)
    new_up_m, new_up_v, new_up_w = adam_update(grad_up[None], up_m, up_v, up_w, 0.02)
    new_prefix_m, new_prefix_v, new_prefix_w = adam_update(
        grad_prefix[None], prefix_m, prefix_v, prefix_w, 2.0
    )

    def group_sum(difference):
        total = difference.astype(jnp.bfloat16)
        bits = 1
        while bits < grp_size:
            other = lax.ppermute(total, "grp", [(j, j ^ bits) for j in range(grp_size)])
            total = total.astype(jnp.float32) + other.astype(jnp.float32)
            bits *= 2
            if bits < grp_size:
                total = total.astype(jnp.bfloat16)
        return total

    summed = (
        group_sum(down_outer - new_down_w[0]),
        group_sum(up_outer - new_up_w[0]),
        group_sum(prefix_outer - new_prefix_w[0]),
    )
    group_count = lax.axis_size("grp")
    outer_results = []
    for outer_weight, momentum, difference in (
        (down_outer, down_mom, summed[0]),
        (up_outer, up_mom, summed[1]),
        (prefix_outer, prefix_mom, summed[2]),
    ):
        average = difference / group_count
        momentum_new = OUTER_MOMENTUM * momentum + average
        outer_results.append(momentum_new)
        outer_results.append(outer_weight - OUTER_RATE * (average + OUTER_MOMENTUM * momentum_new))
    return (
        output[None],
        grad_input[None],
        grad_memory[None],
        grad_down[None],
        grad_up[None],
        grad_prefix[None],
        new_down_m,
        new_down_v,
        new_down_w,
        new_up_m,
        new_up_v,
        new_up_w,
        new_prefix_m,
        new_prefix_v,
        new_prefix_w,
        outer_results[0],
        outer_results[1],
        outer_results[2],
        outer_results[3],
        outer_results[4],
        outer_results[5],
    )


def solution(mesh):
    placed = (
        P("grp", None, None, None),
        P("grp", None, "mem", None),
        P("grp", None, None, None),
        P("grp", None),
        P("grp", None),
        P(),
        P(),
        P(),
        P(),
        P(),
        P(),
        P(),
        P(),
        P("grp", "mem", None),
        P("grp", "mem", None),
        P("grp", None, None, "mem"),
        P("grp", "mem", None),
        P("grp", "mem", None),
        P("grp", "mem", None),
        P("grp", "mem", None),
        P("grp", None, None, "mem"),
        P("grp", None, None, "mem"),
        P("mem", None),
        P("mem", None),
        P(None, None, "mem"),
        P("mem", None),
        P("mem", None),
        P(None, None, "mem"),
    )
    return jax.shard_map(
        local,
        mesh=mesh,
        in_specs=placed,
        out_specs=(
            P("grp", None, None, None),
            P("grp", None, None, None),
            P("grp", None, "mem", None),
            P("grp", "mem", None),
            P("grp", "mem", None),
            P("grp", None, None, "mem"),
            P("grp", "mem", None),
            P("grp", "mem", None),
            P("grp", "mem", None),
            P("grp", "mem", None),
            P("grp", "mem", None),
            P("grp", "mem", None),
            P("grp", None, None, "mem"),
            P("grp", None, None, "mem"),
            P("grp", None, None, "mem"),
            P("mem", None),
            P("mem", None),
            P("mem", None),
            P("mem", None),
            P(None, None, "mem"),
            P(None, None, "mem"),
        ),
        check_vma=False,
    )
```

time: 761 us -> 370 us (0.49)
  matrix products: 266 us -> 102 us
  waiting for transfers between devices: 159 us -> 34.2 us
  blocking collectives: 103 us -> 0 us
  starting transfers between devices: 0.21 us -> 72.7 us
  local copies, waits for them, and re-layouts: 149 us -> 86.4 us
  between operations: 15.2 us -> 2.33 us
    psum x3 -> x0, waiting for transfers between devices: 156 us -> none  [the longest x1 99.4 us: local(): grad_queries = lax.psum(query_part.astype(jnp.bfloat16), 'mem')]
    ppermute x0 -> x66, starting transfers between devices: none -> 72.7 us  [the longest x60 67.7 us: swap(): lax.ppermute(values_in, 'mem', [(j, j ^ bits) for j in range(mem_size)])]
    dot_general x15, matrix products: 93.4 us -> 32.7 us  [the longest x1 6.38 us: local(): jnp.einsum('hqe,khe->hqk', grad_cross, mem_proj[1], preferred_element_typ...]
    psum x2 -> x0, blocking collectives: 46.4 us -> none  [the longest x1 35.4 us: local(): lax.psum((factor * local_sum).astype(jnp.bfloat16), 'mem')]
    dot_general x1, matrix products: 43.9 us -> 2.38 us  [local(): ffn_pre = jnp.dot(normed, ffn_in, preferred_element_type=jnp.float32)]
    reshape x6 -> x0, local copies, waits for them, and re-layouts: 37 us -> none  [the longest x2 12.5 us: local(): grad_cross = jnp.dot(grad_two.astype(jnp.bfloat16), cross_out.T, preferre...]
    ppermute x0 -> x66, waiting for transfers between devices: none -> 34.2 us  [the longest x60 30.7 us: swap(): lax.ppermute(values_in, 'mem', [(j, j ^ bits) for j in range(mem_size)])]
    pmax x1 -> x0, blocking collectives: 33.8 us -> none  [local(): lax.pmax(local_max.astype(jnp.bfloat16), 'mem').astype(local_max.dtype)]
  transfers between devices with their start and end apart: 5 -> 66, of which waited for: 3 -> 16; matrix products, arithmetic and copies ran while one was open for 17% -> 37% of each run, Pallas kernels for 0% -> 0%
where the time goes in v1:
time: 370 us; the launch traced here: 363 us
  matrix products  102 us (28%)
  local copies, waits for them, and re-layouts  86.4 us (23%)
  starting transfers between devices  72.7 us (20%)
  other arithmetic  64.6 us (17%)
  waiting for transfers between devices  34.2 us (9%)
    ppermute x60, starting transfers between devices, swap(): lax.ppermute(values_in, 'mem', [(j, j ^ bits) for j in range(mem_size)])  67.7 us
    ppermute x60, waiting for transfers between devices, swap(): lax.ppermute(values_in, 'mem', [(j, j ^ bits) for j in range(mem_size)])  30.7 us
    dot_general x1, matrix products, local(): jnp.dot(grad_ffn_pre, ffn_in.T, preferred_element_type=jnp.float32)  23.7 us
    unnamed x221, local copies, waits for them, and re-layouts  22.1 us
    unnamed x15, other arithmetic  13.1 us
    another operation x9, other arithmetic, plane_order(): return jnp.take(jnp.stack(pieces), seq ^ jnp.arange(seq_count), axis=0)  11.6 us
    dot_general x1, matrix products, local(): ffn_result = jnp.dot(ffn_act, ffn_out, preferred_element_type=jnp.float32)  10.8 us
    gather x3, local copies, waits for them, and re-layouts, plane_order(): return jnp.take(jnp.stack(pieces), seq ^ jnp.arange(seq_count), axis=0)  9.28 us
  transfers between devices with their start and end apart: 66, of which 16 were waited for; matrix products, arithmetic and copies ran while one was open for 37% of the time, Pallas kernels for 0%

profile of v1, /device:TPU:0, one launch (start us, length us, event | category | flops | bytes accessed | tf_op | source)
XLA Modules:
  0.0 362.9 jit_solution(13056965737721048843)
XLA Ops:
  0.7 2.0 dynamic-slice_bitcast_fusion.12
  2.7 3.0 collective-permute-start.3
  5.7 2.5 collective-permute-start.7
  19.7 4.8 %fusion.34 = bf16[3,256,1024]{2,1,0:T(8,128)(2,1)S(1)} fusion(bf16[3,1024,1024]{2,1,0:T(8,128)(2,1)} %param.37, bf16[1,4,256,1024]{3,2,1,0:T(8,128)(2,1)} %param.32, s32[]{:T(128)S(6)} %select_n.161), kind=kOutput, calls=%fused_computation.69 | convolution fusion | flops 1611399168 | bytes 8388612 | tf_op jit(solution)/shard_map/rd,cde->cre/dot_general | solution.py:176
  36.1 2.2 copy.72
  40.0 2.9 collective-permute-done.24
  50.3 2.1 collective-permute-done.11
  58.8 5.2 %collective-permute-done.2 = bf16[2,30,512]{2,0,1:T(2,128)(2,1)S(1)} collective-permute-done((bf16[2,30,512]{2,0,1:T(2,128)(2,1)S(1)}, bf16[2,30,512]{2,0,1:T(2,128)(2,1)S(1)}, u32[]{:S(2)}, u32[]{:S(2)}) %collective-permute-start.2) | collective-permute-done | bytes 61472 | tf_op jit(solution)/shard_map/ppermute | solution.py:112
  78.0 2.4 fusion.54
  90.7 6.6 %collective-permute-done.6 = bf16[64,1024]{1,0:T(8,128)(2,1)S(1)} collective-permute-done((bf16[64,1024]{1,0:T(8,128)(2,1)S(1)}, bf16[64,1024]{1,0:T(8,128)(2,1)S(1)}, u32[]{:S(2)}, u32[]{:S(2)}) %collective-permute-start.6) | collective-permute-done | bytes 131104 | tf_op jit(solution)/shard_map/ppermute | solution.py:112
  99.7 2.1 collective-permute-done.27
  102.3 2.1 collective-permute-start.14
  130.3 2.9 gather_fusion.3
  133.2 2.4 broadcast_select_fusion
  135.7 4.5 %convert_bitcast_fusion = bf16[2,512,1024]{2,1,0:T(8,128)(2,1)S(1)} fusion(bf16[512,1024,1]{1,0,2:T(8,128)(2,1)S(1)} %bitcast.369, bf16[3,1024,1024]{2,1,0:T(8,128)(2,1)} %param.39), kind=kOutput, calls=%fused_computation.56 | convolution fusion | flops 2148532224 | bytes 7340032 | tf_op jit(solution)/shard_map/rd,cde->cre/dot_general | solution.py:210
  143.2 2.6 copy.78
  145.9 2.6 fusion.1
  148.5 2.7 convert_reduce_fusion
  151.8 2.4 fusion.78
  156.9 2.9 gather_fusion
  162.4 2.2 multiply_convert_fusion.8
  164.9 2.4 fusion.191
  167.7 10.8 %fusion.50 = f32[256,1024]{1,0:T(8,128)S(1)} fusion(bf16[4096,1024]{1,0:T(8,128)(2,1)S(1)} %bitcast.410, f32[256,4096]{1,0:T(8,128)S(1)} %fusion.191, f32[256,1024]{1,0:T(8,128)S(1)} %get-tuple-element.112, f32[1024]{0:T(1024)S(1)} %bitcast.406, f32[1024]{0:T(1024)S(1)} %bitcast.397, f32[256]{0:T(256)S(1)} %add_rsqrt_fusion.1, ...), kind=kOutput, calls=%fused_computation.86 | convolution fusion | flops 2216951808 | bytes 14690304 | tf_op jit(solution)/shard_map/dot_general | solution.py:236
  180.2 2.3 fusion.74
  182.5 23.7 %fusion.49 = f32[256,1024]{1,0:T(8,128)} fusion(bf16[1024,4096]{1,0:T(8,128)(2,1)} %param.41, f32[256,4096]{1,0:T(8,128)} %copy-done.99, bf16[4096,1024]{1,0:T(8,128)(2,1)} %param.42, f32[256]{0:T(256)S(1)} %broadcast_multiply_fusion.4, f32[256,1024]{1,0:T(8,128)} %copy-done.8, f32[256]{0:T(256)S(1)} %broadcast_multiply_fusion.6, ...), kind=kOutput, calls=%fused_computation.83 | convolution fusion | flops 4375707648 | bytes 25185280 | tf_op jit(solution)/shard_map/dot_general | solution.py:272
  206.3 3.7 %add_convert_fusion.5 = bf16[256,512]{1,0:T(8,128)(2,1)S(1)} fusion(f32[256,512]{1,0:T(8,128)} %get-tuple-element.114, bf16[512,1024]{1,0:T(8,128)(2,1)} %bitcast.354, f32[256,1024]{1,0:T(8,128)} %copy-done.8, f32[256]{0:T(256)S(1)} %broadcast_multiply_fusion.4, f32[256]{0:T(256)S(1)} %broadcast_multiply_fusion.5, f32[256]{0:T(256)S(1)} %copy-done.88, ...), kind=kOutput, calls=%fused_computation.149 | convolution fusion | flops 280756224 | bytes 3417092 | tf_op jit(solution)/shard_map/dot_general | solution.py:251
  213.3 2.0 copy.79
  216.9 6.4 %multiply_convert_fusion = bf16[16,256,512]{2,1,0:T(8,128)(2,1)S(1)} fusion(f32[16,256,512]{2,1,0:T(8,128)} %copy-done.1, f32[16,256]{1,0:T(8,128)S(1)} %fusion.67, f32[16,256]{1,0:T(8,128)S(1)} %get-tuple-element.54, f32[16,256]{1,0:T(8,128)S(1)} %get-tuple-element.107, pred[512]{0:T(512)(128)(4,1)S(1)} %copy-done.86, bf16[16,256,64]{1,2,0:T(8,128)(2,1)} %bitcast.360, ...), kind=kOutput, calls=%fused_computation.7 | convolution fusion | flops 283115520 | bytes 14205440 | tf_op jit(solution)/shard_map/hqe,khe->hqk/dot_general | solution.py:282
  226.4 2.8 fusion.170
  231.9 2.1 copy.80
  234.0 4.0 %multiply_reduce_fusion = (f32[16,256]{1,0:T(8,128)S(1)}, f32[16,256,286]{1,2,0:T(8,128)S(1)}) fusion(f32[16,256,286]{1,2,0:T(8,128)} %copy-done.17, f32[16,256]{1,0:T(8,128)S(1)} %copy-done.79, bf16[256,16,64]{0,2,1:T(8,128)(2,1)} %bitcast.377, bf16[256,16,64]{0,2,1:T(8,128)(2,1)S(1)} %bitcast.375, bf16[30,16,64]{0,2,1:T(8,128)(2,1)} %bitcast.385), kind=kOutput, calls=%fused_computation.15 | convolution fusion | flops 154628096 | bytes 10514432 | tf_op jit(solution)/shard_map/qhe,khe->hqk/dot_general | solution.py:330
  264.7 2.3 copy.85
  267.0 2.4 copy.84
  271.3 2.1 copy.82
  273.4 2.0 copy.83
  275.5 3.9 %fusion.62 = bf16[256,1024]{1,0:T(8,128)(2,1)S(1)} fusion(bf16[3,1024,1024]{2,1,0:T(8,128)(2,1)} %param.39, s32[]{:T(128)S(6)} %select_n.178, bf16[1,512,1024]{2,1,0:T(8,128)(2,1)} %copy.84, bf16[1,512,1024]{2,1,0:T(8,128)(2,1)} %copy.85), kind=kOutput, calls=%fused_computation.95 | convolution fusion | flops 1076101120 | bytes 6815748 | tf_op jit(solution)/shard_map/cre,cde->rd/dot_general | solution.py:315
  279.6 5.0 %fusion.57 = bf16[256,1024]{1,0:T(8,128)(2,1)S(1)} fusion(bf16[3,1024,1024]{2,1,0:T(8,128)(2,1)} %param.37, bf16[1,256,1024]{2,1,0:T(8,128)(2,1)S(1)} %copy-done.51, bf16[1,256,1024]{2,1,0:T(8,128)(2,1)S(1)} %copy-done.50, bf16[1,256,1024]{2,1,0:T(8,128)(2,1)S(1)} %copy-done.49, f32[256]{0:T(256)S(1)} %copy-done.93, f32[256,1024]{1,0:T(8,128)S(1)} %copy-done.7, ...), kind=kOutput, calls=%fused_computation.92 | convolution fusion | flops 1614282752 | bytes 10489856 | tf_op jit(solution)/shard_map/cre,cde->rd/dot_general | solution.py:356
  291.0 2.2 collective-permute-done.65
  293.1 2.9 collective-permute-start.50
  300.2 2.1 collective-permute-start.49
  302.3 2.2 fusion.113
  312.8 2.5 fusion.114
  328.6 3.5 collective-permute-done.45
  341.5 3.0 collective-permute-done.41
  346.1 3.8 %gather_fusion.4 = bf16[4,256,1024]{2,1,0:T(8,128)(2,1)} fusion(bf16[4,256,1024]{2,1,0:T(8,128)(2,1)} %pad_maximum_fusion, s32[1024]{0:T(1024)} %pad_clamp_fusion.1), kind=kCustom, calls=%fused_computation.1.clone | custom fusion | bytes 4194320 | tf_op jit(solution)/shard_map/jit(_take)/gather | solution.py:134
  350.9 2.6 pad_maximum_fusion.1
  353.5 3.8 %gather_fusion.5 = bf16[4,256,1024]{2,1,0:T(8,128)(2,1)} fusion(bf16[4,256,1024]{2,1,0:T(8,128)(2,1)} %pad_maximum_fusion.1, s32[1024]{0:T(1024)} %pad_clamp_fusion.1), kind=kCustom, calls=%fused_computation.3.clone | custom fusion | bytes 4194320 | tf_op jit(solution)/shard_map/jit(_take)/gather | solution.py:134
  357.3 5.4 %bitcast_convert_fusion = (f32[1,4,256,1024]{3,2,1,0:T(8,128)}, bf16[1,4,256,1024]{3,2,1,0:T(8,128)(2,1)}) fusion(bf16[4,256,1024]{2,1,0:T(8,128)(2,1)} %gather_fusion.5, pred[4]{0:T(512)(128)(4,1)S(1)} %copy-done.87, bf16[4,256,1024]{2,1,0:T(8,128)(2,1)} %gather_fusion.4), kind=kLoop, calls=%fused_computation.48 | loop fusion | flops 3145728 | bytes 10485764 | tf_op jit(solution)/shard_map/broadcast_in_dim | solution.py:408
  (465 shorter events, 185.3 us)
Async XLA Ops:
  2.7 78.6 %collective-permute-start.3 = (bf16[64,1024]{1,0:T(8,128)(2,1)}, bf16[64,1024]{1,0:T(8,128)(2,1)}, u32[]{:S(2)}, u32[]{:S(2)}) collective-permute-start(bf16[64,1024]{1,0:T(8,128)(2,1)} %get-tuple-element.77), channel_id=1, source_target_pairs={{0,1},{1,0},{2,3},{3,2},{4,5},{5,4},{6,7},{7,6},{8,9},{9,8},{10,11... | collective-permute-start | bytes 393224 | tf_op jit(solution)/shard_map/ppermute | solution.py:112
  5.7 92.3 %collective-permute-start.7 = (bf16[64,1024]{1,0:T(8,128)(2,1)}, bf16[64,1024]{1,0:T(8,128)(2,1)}, u32[]{:S(2)}, u32[]{:S(2)}) collective-permute-start(bf16[64,1024]{1,0:T(8,128)(2,1)} %get-tuple-element.77), channel_id=1, source_target_pairs={{0,5},{1,4},{2,7},{3,6},{4,1},{5,0},{6,3},{7,2},{8,13},{9,12},{10,... | collective-permute-start | bytes 393224 | tf_op jit(solution)/shard_map/ppermute | solution.py:112
  10.5 33.9 %collective-permute-start.23 = (bf16[32,1024]{1,0:T(8,128)(2,1)}, bf16[32,1024]{1,0:T(8,128)(2,1)}, u32[]{:S(2)}, u32[]{:S(2)}) collective-permute-start(bf16[32,1024]{1,0:T(8,128)(2,1)} %get-tuple-element.82), channel_id=1, source_target_pairs={{0,1},{1,0},{2,3},{3,2},{4,5},{5,4},{6,7},{7,6},{8,9},{9,8},{10,11... | collective-permute-start | bytes 196616 | tf_op jit(solution)/shard_map/ppermute | solution.py:112
  12.1 35.4 %collective-permute-start.25 = (bf16[32,1024]{1,0:T(8,128)(2,1)}, bf16[32,1024]{1,0:T(8,128)(2,1)}, u32[]{:S(2)}, u32[]{:S(2)}) collective-permute-start(bf16[32,1024]{1,0:T(8,128)(2,1)} %get-tuple-element.82), channel_id=1, source_target_pairs={{0,2},{1,3},{2,0},{3,1},{4,6},{5,7},{6,4},{7,5},{8,10},{9,11},{10,... | collective-permute-start | bytes 196616 | tf_op jit(solution)/shard_map/ppermute | solution.py:112
  14.4 18.2 %collective-permute-start = (bf16[2,30,128]{2,0,1:T(2,128)(2,1)S(1)}, bf16[2,30,128]{2,0,1:T(2,128)(2,1)S(1)}, u32[]{:S(2)}, u32[]{:S(2)}) collective-permute-start(bf16[2,30,128]{2,0,1:T(2,128)(2,1)S(1)} %convert_bitcast_fusion.1), channel_id=1, source_target_pairs={{0,1},{1,0},{2,3},{3,2},{4,5},{5,4},{6,7},{7,6},{8,9},{9,8},{10,11... | collective-permute-start | bytes 46088 | tf_op jit(solution)/shard_map/ppermute | solution.py:112
  44.4 9.5 %collective-permute-start.10 = (bf16[64,512]{1,0:T(8,128)(2,1)}, bf16[64,512]{1,0:T(8,128)(2,1)S(1)}, u32[]{:S(2)}, u32[]{:S(2)}) collective-permute-start(bf16[64,512]{1,0:T(8,128)(2,1)} %get-tuple-element.86), channel_id=1, source_target_pairs={{0,1},{1,0},{2,3},{3,2},{4,5},{5,4},{6,7},{7,6},{8,9},{9,8},{10,11... | collective-permute-start | bytes 196616 | tf_op jit(solution)/shard_map/ppermute | solution.py:112
  47.5 7.6 %collective-permute-start.12 = (bf16[64,512]{1,0:T(8,128)(2,1)}, bf16[64,512]{1,0:T(8,128)(2,1)S(1)}, u32[]{:S(2)}, u32[]{:S(2)}) collective-permute-start(bf16[64,512]{1,0:T(8,128)(2,1)} %get-tuple-element.86), channel_id=1, source_target_pairs={{0,2},{1,3},{2,0},{3,1},{4,6},{5,7},{6,4},{7,5},{8,10},{9,11},{10,... | collective-permute-start | bytes 196616 | tf_op jit(solution)/shard_map/ppermute | solution.py:112
  54.0 30.6 %collective-permute-start.4 = (bf16[64,1024]{1,0:T(8,128)(2,1)}, bf16[64,1024]{1,0:T(8,128)(2,1)}, u32[]{:S(2)}, u32[]{:S(2)}) collective-permute-start(bf16[64,1024]{1,0:T(8,128)(2,1)} %get-tuple-element.79), channel_id=1, source_target_pairs={{0,2},{1,3},{2,0},{3,1},{4,6},{5,7},{6,4},{7,5},{8,10},{9,11},{10,... | collective-permute-start | bytes 393224 | tf_op jit(solution)/shard_map/ppermute | solution.py:112
  55.1 50.7 %collective-permute-start.8 = (bf16[64,1024]{1,0:T(8,128)(2,1)}, bf16[64,1024]{1,0:T(8,128)(2,1)}, u32[]{:S(2)}, u32[]{:S(2)}) collective-permute-start(bf16[64,1024]{1,0:T(8,128)(2,1)} %get-tuple-element.79), channel_id=1, source_target_pairs={{0,6},{1,7},{2,4},{3,5},{4,2},{5,3},{6,0},{7,1},{8,14},{9,15},{10,... | collective-permute-start | bytes 393224 | tf_op jit(solution)/shard_map/ppermute | solution.py:112
  64.0 23.9 %collective-permute-start.5 = (bf16[64,1024]{1,0:T(8,128)(2,1)}, bf16[64,1024]{1,0:T(8,128)(2,1)}, u32[]{:S(2)}, u32[]{:S(2)}) collective-permute-start(bf16[64,1024]{1,0:T(8,128)(2,1)} %get-tuple-element.78), channel_id=1, source_target_pairs={{0,3},{1,2},{2,1},{3,0},{4,7},{5,6},{6,5},{7,4},{8,11},{9,10},{10,... | collective-permute-start | bytes 393224 | tf_op jit(solution)/shard_map/ppermute | solution.py:112
  81.4 32.2 %collective-permute-start.9 = (bf16[64,1024]{1,0:T(8,128)(2,1)S(1)}, bf16[64,1024]{1,0:T(8,128)(2,1)S(1)}, u32[]{:S(2)}, u32[]{:S(2)}) collective-permute-start(bf16[64,1024]{1,0:T(8,128)(2,1)S(1)} %copy-done.62), channel_id=1, source_target_pairs={{0,7},{1,6},{2,5},{3,4},{4,3},{5,2},{6,1},{7,0},{8,15},{9,14},{10,... | collective-permute-start | bytes 393224 | tf_op jit(solution)/shard_map/ppermute | solution.py:112
  84.6 12.7 %collective-permute-start.6 = (bf16[64,1024]{1,0:T(8,128)(2,1)S(1)}, bf16[64,1024]{1,0:T(8,128)(2,1)S(1)}, u32[]{:S(2)}, u32[]{:S(2)}) collective-permute-start(bf16[64,1024]{1,0:T(8,128)(2,1)S(1)} %copy-done.63), channel_id=1, source_target_pairs={{0,4},{1,5},{2,6},{3,7},{4,0},{5,1},{6,2},{7,3},{8,12},{9,13},{10,... | collective-permute-start | bytes 393224 | tf_op jit(solution)/shard_map/ppermute | solution.py:112
  88.0 17.2 %collective-permute-start.29 = (bf16[64,1024]{1,0:T(8,128)(2,1)S(1)}, bf16[64,1024]{1,0:T(8,128)(2,1)S(1)}, u32[]{:S(2)}, u32[]{:S(2)}) collective-permute-start(bf16[64,1024]{1,0:T(8,128)(2,1)S(1)} %bitcast.379), channel_id=1, source_target_pairs={{0,4},{1,5},{2,6},{3,7},{4,0},{5,1},{6,2},{7,3},{8,12},{9,13},{10,... | collective-permute-start | bytes 393224 | tf_op jit(solution)/shard_map/ppermute | solution.py:112
  101.8 10.4 %collective-permute-start.16 = (bf16[128,512]{1,0:T(8,128)(2,1)S(1)}, bf16[128,512]{1,0:T(8,128)(2,1)S(1)}, u32[]{:S(2)}, u32[]{:S(2)}) collective-permute-start(bf16[128,512]{1,0:T(8,128)(2,1)S(1)} %bitcast.380), channel_id=1, source_target_pairs={{0,4},{1,5},{2,6},{3,7},{4,0},{5,1},{6,2},{7,3},{8,12},{9,13},{10,... | collective-permute-start | bytes 393224 | tf_op jit(solution)/shard_map/ppermute | solution.py:112
  105.8 12.7 %collective-permute-start.30 = (bf16[32,1024]{1,0:T(8,128)(2,1)S(1)}, bf16[32,1024]{1,0:T(8,128)(2,1)}, u32[]{:S(2)}, u32[]{:S(2)}) collective-permute-start(bf16[32,1024]{1,0:T(8,128)(2,1)S(1)} %get-tuple-element.80), channel_id=1, source_target_pairs={{0,1},{1,0},{2,3},{3,2},{4,5},{5,4},{6,7},{7,6},{8,9},{9,8},{10,11... | collective-permute-start | bytes 196616 | tf_op jit(solution)/shard_map/ppermute | solution.py:112
  108.0 13.7 %collective-permute-start.32 = (bf16[32,1024]{1,0:T(8,128)(2,1)S(1)}, bf16[32,1024]{1,0:T(8,128)(2,1)S(1)}, u32[]{:S(2)}, u32[]{:S(2)}) collective-permute-start(bf16[32,1024]{1,0:T(8,128)(2,1)S(1)} %get-tuple-element.80), channel_id=1, source_target_pairs={{0,2},{1,3},{2,0},{3,1},{4,6},{5,7},{6,4},{7,5},{8,10},{9,11},{10,... | collective-permute-start | bytes 196616 | tf_op jit(solution)/shard_map/ppermute | solution.py:112
  112.2 9.7 %collective-permute-start.33 = (bf16[32,1024]{1,0:T(8,128)(2,1)S(1)}, bf16[32,1024]{1,0:T(8,128)(2,1)}, u32[]{:S(2)}, u32[]{:S(2)}) collective-permute-start(bf16[32,1024]{1,0:T(8,128)(2,1)S(1)} %get-tuple-element.81), channel_id=1, source_target_pairs={{0,2},{1,3},{2,0},{3,1},{4,6},{5,7},{6,4},{7,5},{8,10},{9,11},{10,... | collective-permute-start | bytes 196616 | tf_op jit(solution)/shard_map/ppermute | solution.py:112
  113.6 13.8 %collective-permute-start.17 = (bf16[64,512]{1,0:T(8,128)(2,1)}, bf16[64,512]{1,0:T(8,128)(2,1)}, u32[]{:S(2)}, u32[]{:S(2)}) collective-permute-start(bf16[64,512]{1,0:T(8,128)(2,1)} %get-tuple-element.84), channel_id=1, source_target_pairs={{0,1},{1,0},{2,3},{3,2},{4,5},{5,4},{6,7},{7,6},{8,9},{9,8},{10,11... | collective-permute-start | bytes 196616 | tf_op jit(solution)/shard_map/ppermute | solution.py:112
  116.7 8.9 %collective-permute-start.19 = (bf16[64,512]{1,0:T(8,128)(2,1)}, bf16[64,512]{1,0:T(8,128)(2,1)S(1)}, u32[]{:S(2)}, u32[]{:S(2)}) collective-permute-start(bf16[64,512]{1,0:T(8,128)(2,1)} %get-tuple-element.84), channel_id=1, source_target_pairs={{0,2},{1,3},{2,0},{3,1},{4,6},{5,7},{6,4},{7,5},{8,10},{9,11},{10,... | collective-permute-start | bytes 196616 | tf_op jit(solution)/shard_map/ppermute | solution.py:112
  121.8 7.2 %collective-permute-start.20 = (bf16[64,512]{1,0:T(8,128)(2,1)}, bf16[64,512]{1,0:T(8,128)(2,1)S(1)}, u32[]{:S(2)}, u32[]{:S(2)}) collective-permute-start(bf16[64,512]{1,0:T(8,128)(2,1)} %get-tuple-element.85), channel_id=1, source_target_pairs={{0,2},{1,3},{2,0},{3,1},{4,6},{5,7},{6,4},{7,5},{8,10},{9,11},{10,... | collective-permute-start | bytes 196616 | tf_op jit(solution)/shard_map/ppermute | solution.py:112
  121.9 7.7 %collective-permute-start.34 = (bf16[32,1024]{1,0:T(8,128)(2,1)S(1)}, bf16[32,1024]{1,0:T(8,128)(2,1)S(1)}, u32[]{:S(2)}, u32[]{:S(2)}) collective-permute-start(bf16[32,1024]{1,0:T(8,128)(2,1)S(1)} %collective-permute-done.32), channel_id=1, source_target_pairs={{0,1},{1,0},{2,3},{3,2},{4,5},{5,4},{6,7},{7,6},{8,9},{9,8},{10,11... | collective-permute-start | bytes 196616 | tf_op jit(solution)/shard_map/ppermute | solution.py:112
  125.6 29.7 %collective-permute-start.21 = (bf16[64,512]{1,0:T(8,128)(2,1)S(1)}, bf16[64,512]{1,0:T(8,128)(2,1)S(1)}, u32[]{:S(2)}, u32[]{:S(2)}) collective-permute-start(bf16[64,512]{1,0:T(8,128)(2,1)S(1)} %collective-permute-done.19), channel_id=1, source_target_pairs={{0,1},{1,0},{2,3},{3,2},{4,5},{5,4},{6,7},{7,6},{8,9},{9,8},{10,11... | collective-permute-start | bytes 196616 | tf_op jit(solution)/shard_map/ppermute | solution.py:112
  127.4 28.0 %collective-permute-start.22 = (bf16[64,512]{1,0:T(8,128)(2,1)S(1)}, bf16[64,512]{1,0:T(8,128)(2,1)}, u32[]{:S(2)}, u32[]{:S(2)}) collective-permute-start(bf16[64,512]{1,0:T(8,128)(2,1)S(1)} %collective-permute-done.18), channel_id=1, source_target_pairs={{0,2},{1,3},{2,0},{3,1},{4,6},{5,7},{6,4},{7,5},{8,10},{9,11},{10,... | collective-permute-start | bytes 196616 | tf_op jit(solution)/shard_map/ppermute | solution.py:112
  255.4 30.0 %collective-permute-start.57 = (bf16[2,30,128]{2,0,1:T(2,128)(2,1)}, bf16[2,30,128]{2,0,1:T(2,128)(2,1)S(1)}, u32[]{:S(2)}, u32[]{:S(2)}) collective-permute-start(bf16[2,30,128]{2,0,1:T(2,128)(2,1)} %get-tuple-element.90), channel_id=1, source_target_pairs={{0,1},{1,0},{2,3},{3,2},{4,5},{5,4},{6,7},{7,6},{8,9},{9,8},{10,11... | collective-permute-start | bytes 46088 | tf_op jit(solution)/shard_map/ppermute | solution.py:112
  256.0 30.7 %collective-permute-start.58 = (bf16[2,30,128]{2,0,1:T(2,128)(2,1)S(1)}, bf16[2,30,128]{2,0,1:T(2,128)(2,1)S(1)}, u32[]{:S(2)}, u32[]{:S(2)}) collective-permute-start(bf16[2,30,128]{2,0,1:T(2,128)(2,1)S(1)} %get-tuple-element.92), channel_id=1, source_target_pairs={{0,2},{1,3},{2,0},{3,1},{4,6},{5,7},{6,4},{7,5},{8,10},{9,11},{10,... | collective-permute-start | bytes 46088 | tf_op jit(solution)/shard_map/ppermute | solution.py:112
  257.7 29.5 %collective-permute-start.59 = (bf16[2,30,128]{2,0,1:T(2,128)(2,1)S(1)}, bf16[2,30,128]{2,0,1:T(2,128)(2,1)S(1)}, u32[]{:S(2)}, u32[]{:S(2)}) collective-permute-start(bf16[2,30,128]{2,0,1:T(2,128)(2,1)S(1)} %get-tuple-element.91), channel_id=1, source_target_pairs={{0,3},{1,2},{2,1},{3,0},{4,7},{5,6},{6,5},{7,4},{8,11},{9,10},{10,... | collective-permute-start | bytes 46088 | tf_op jit(solution)/shard_map/ppermute | solution.py:112
  261.6 35.1 %collective-permute-start.54 = (bf16[64,1024]{1,0:T(8,128)(2,1)}, bf16[64,1024]{1,0:T(8,128)(2,1)}, u32[]{:S(2)}, u32[]{:S(2)}) collective-permute-start(bf16[64,1024]{1,0:T(8,128)(2,1)} %get-tuple-element.62), channel_id=1, source_target_pairs={{0,1},{1,0},{2,3},{3,2},{4,5},{5,4},{6,7},{7,6},{8,9},{9,8},{10,11... | collective-permute-start | bytes 393224 | tf_op jit(solution)/shard_map/ppermute | solution.py:112
  262.1 34.6 %collective-permute-start.55 = (bf16[64,1024]{1,0:T(8,128)(2,1)}, bf16[64,1024]{1,0:T(8,128)(2,1)}, u32[]{:S(2)}, u32[]{:S(2)}) collective-permute-start(bf16[64,1024]{1,0:T(8,128)(2,1)} %get-tuple-element.64), channel_id=1, source_target_pairs={{0,2},{1,3},{2,0},{3,1},{4,6},{5,7},{6,4},{7,5},{8,10},{9,11},{10,... | collective-permute-start | bytes 393224 | tf_op jit(solution)/shard_map/ppermute | solution.py:112
  285.5 13.0 %collective-permute-start.56 = (bf16[64,1024]{1,0:T(8,128)(2,1)}, bf16[64,1024]{1,0:T(8,128)(2,1)S(1)}, u32[]{:S(2)}, u32[]{:S(2)}) collective-permute-start(bf16[64,1024]{1,0:T(8,128)(2,1)} %get-tuple-element.63), channel_id=1, source_target_pairs={{0,3},{1,2},{2,1},{3,0},{4,7},{5,6},{6,5},{7,4},{8,11},{9,10},{10,... | collective-permute-start | bytes 393224 | tf_op jit(solution)/shard_map/ppermute | solution.py:112
  286.6 24.9 %collective-permute-start.51 = (bf16[128,512]{1,0:T(8,128)(2,1)}, bf16[128,512]{1,0:T(8,128)(2,1)}, u32[]{:S(2)}, u32[]{:S(2)}) collective-permute-start(bf16[128,512]{1,0:T(8,128)(2,1)} %get-tuple-element.65), channel_id=1, source_target_pairs={{0,1},{1,0},{2,3},{3,2},{4,5},{5,4},{6,7},{7,6},{8,9},{9,8},{10,11... | collective-permute-start | bytes 393224 | tf_op jit(solution)/shard_map/ppermute | solution.py:112
  296.7 15.4 %collective-permute-start.52 = (bf16[128,512]{1,0:T(8,128)(2,1)}, bf16[128,512]{1,0:T(8,128)(2,1)}, u32[]{:S(2)}, u32[]{:S(2)}) collective-permute-start(bf16[128,512]{1,0:T(8,128)(2,1)} %get-tuple-element.67), channel_id=1, source_target_pairs={{0,2},{1,3},{2,0},{3,1},{4,6},{5,7},{6,4},{7,5},{8,10},{9,11},{10,... | collective-permute-start | bytes 393224 | tf_op jit(solution)/shard_map/ppermute | solution.py:112
  296.7 16.0 %collective-permute-start.53 = (bf16[128,512]{1,0:T(8,128)(2,1)}, bf16[128,512]{1,0:T(8,128)(2,1)}, u32[]{:S(2)}, u32[]{:S(2)}) collective-permute-start(bf16[128,512]{1,0:T(8,128)(2,1)} %get-tuple-element.66), channel_id=1, source_target_pairs={{0,3},{1,2},{2,1},{3,0},{4,7},{5,6},{6,5},{7,4},{8,11},{9,10},{10,... | collective-permute-start | bytes 393224 | tf_op jit(solution)/shard_map/ppermute | solution.py:112
  298.5 7.1 %collective-permute-start.48 = (bf16[64,1024]{1,0:T(8,128)(2,1)S(1)}, bf16[64,1024]{1,0:T(8,128)(2,1)S(1)}, u32[]{:S(2)}, u32[]{:S(2)}) collective-permute-start(bf16[64,1024]{1,0:T(8,128)(2,1)S(1)} %get-tuple-element.71), channel_id=1, source_target_pairs={{0,1},{1,0},{2,3},{3,2},{4,5},{5,4},{6,7},{7,6},{8,9},{9,8},{10,11... | collective-permute-start | bytes 393224 | tf_op jit(solution)/shard_map/ppermute | solution.py:112
  300.2 7.2 %collective-permute-start.49 = (bf16[64,1024]{1,0:T(8,128)(2,1)S(1)}, bf16[64,1024]{1,0:T(8,128)(2,1)S(1)}, u32[]{:S(2)}, u32[]{:S(2)}) collective-permute-start(bf16[64,1024]{1,0:T(8,128)(2,1)S(1)} %get-tuple-element.70), channel_id=1, source_target_pairs={{0,2},{1,3},{2,0},{3,1},{4,6},{5,7},{6,4},{7,5},{8,10},{9,11},{10,... | collective-permute-start | bytes 393224 | tf_op jit(solution)/shard_map/ppermute | solution.py:112
  305.5 13.7 %collective-permute-start.36 = (bf16[128,1024]{1,0:T(8,128)(2,1)}, bf16[128,1024]{1,0:T(8,128)(2,1)}, u32[]{:S(2)}, u32[]{:S(2)}) collective-permute-start(bf16[128,1024]{1,0:T(8,128)(2,1)} %get-tuple-element.74), channel_id=1, source_target_pairs={{0,1},{1,0},{2,3},{3,2},{4,5},{5,4},{6,7},{7,6},{8,9},{9,8},{10,11... | collective-permute-start | bytes 786440 | tf_op jit(solution)/shard_map/ppermute | solution.py:112
  307.4 14.0 %collective-permute-start.38 = (bf16[128,1024]{1,0:T(8,128)(2,1)}, bf16[128,1024]{1,0:T(8,128)(2,1)}, u32[]{:S(2)}, u32[]{:S(2)}) collective-permute-start(bf16[128,1024]{1,0:T(8,128)(2,1)} %get-tuple-element.74), channel_id=1, source_target_pairs={{0,2},{1,3},{2,0},{3,1},{4,6},{5,7},{6,4},{7,5},{8,10},{9,11},{10,... | collective-permute-start | bytes 786440 | tf_op jit(solution)/shard_map/ppermute | solution.py:112
  311.5 8.4 %collective-permute-start.37 = (bf16[128,1024]{1,0:T(8,128)(2,1)}, bf16[128,1024]{1,0:T(8,128)(2,1)S(1)}, u32[]{:S(2)}, u32[]{:S(2)}) collective-permute-start(bf16[128,1024]{1,0:T(8,128)(2,1)} %get-tuple-element.75), channel_id=1, source_target_pairs={{0,1},{1,0},{2,3},{3,2},{4,5},{5,4},{6,7},{7,6},{8,9},{9,8},{10,11... | collective-permute-start | bytes 786440 | tf_op jit(solution)/shard_map/ppermute | solution.py:112
  312.1 11.0 %collective-permute-start.39 = (bf16[128,1024]{1,0:T(8,128)(2,1)}, bf16[128,1024]{1,0:T(8,128)(2,1)S(1)}, u32[]{:S(2)}, u32[]{:S(2)}) collective-permute-start(bf16[128,1024]{1,0:T(8,128)(2,1)} %get-tuple-element.75), channel_id=1, source_target_pairs={{0,2},{1,3},{2,0},{3,1},{4,6},{5,7},{6,4},{7,5},{8,10},{9,11},{10,... | collective-permute-start | bytes 786440 | tf_op jit(solution)/shard_map/ppermute | solution.py:112
  317.8 9.2 %collective-permute-start.44 = (bf16[128,1024]{1,0:T(8,128)(2,1)S(1)}, bf16[128,1024]{1,0:T(8,128)(2,1)}, u32[]{:S(2)}, u32[]{:S(2)}) collective-permute-start(bf16[128,1024]{1,0:T(8,128)(2,1)S(1)} %copy-done.61), channel_id=1, source_target_pairs={{0,2},{1,3},{2,0},{3,1},{4,6},{5,7},{6,4},{7,5},{8,10},{9,11},{10,... | collective-permute-start | bytes 786440 | tf_op jit(solution)/shard_map/ppermute | solution.py:112
  319.2 12.8 %collective-permute-start.45 = (bf16[128,1024]{1,0:T(8,128)(2,1)S(1)}, bf16[128,1024]{1,0:T(8,128)(2,1)S(1)}, u32[]{:S(2)}, u32[]{:S(2)}) collective-permute-start(bf16[128,1024]{1,0:T(8,128)(2,1)S(1)} %get-tuple-element.73), channel_id=1, source_target_pairs={{0,2},{1,3},{2,0},{3,1},{4,6},{5,7},{6,4},{7,5},{8,10},{9,11},{10,... | collective-permute-start | bytes 786440 | tf_op jit(solution)/shard_map/ppermute | solution.py:112
  319.9 15.3 %collective-permute-start.42 = (bf16[128,1024]{1,0:T(8,128)(2,1)S(1)}, bf16[128,1024]{1,0:T(8,128)(2,1)S(1)}, u32[]{:S(2)}, u32[]{:S(2)}) collective-permute-start(bf16[128,1024]{1,0:T(8,128)(2,1)S(1)} %copy-done.61), channel_id=1, source_target_pairs={{0,1},{1,0},{2,3},{3,2},{4,5},{5,4},{6,7},{7,6},{8,9},{9,8},{10,11... | collective-permute-start | bytes 786440 | tf_op jit(solution)/shard_map/ppermute | solution.py:112
  321.4 15.3 %collective-permute-start.43 = (bf16[128,1024]{1,0:T(8,128)(2,1)S(1)}, bf16[128,1024]{1,0:T(8,128)(2,1)}, u32[]{:S(2)}, u32[]{:S(2)}) collective-permute-start(bf16[128,1024]{1,0:T(8,128)(2,1)S(1)} %get-tuple-element.73), channel_id=1, source_target_pairs={{0,1},{1,0},{2,3},{3,2},{4,5},{5,4},{6,7},{7,6},{8,9},{9,8},{10,11... | collective-permute-start | bytes 786440 | tf_op jit(solution)/shard_map/ppermute | solution.py:112
  323.0 16.0 %collective-permute-start.63 = (bf16[64,1024]{1,0:T(8,128)(2,1)S(1)}, bf16[64,1024]{1,0:T(8,128)(2,1)S(1)}, u32[]{:S(2)}, u32[]{:S(2)}) collective-permute-start(bf16[64,1024]{1,0:T(8,128)(2,1)S(1)} %add_convert_fusion.6), channel_id=1, source_target_pairs={{0,16},{8,24},{16,0},{24,8},{1,17},{9,25},{17,1},{25,9},{2,18},{10... | collective-permute-start | bytes 393224 | tf_op jit(solution)/shard_map/ppermute | solution.py:383
  327.1 13.5 %collective-permute-start.61 = (bf16[128,512]{1,0:T(8,128)(2,1)S(1)}, bf16[128,512]{1,0:T(8,128)(2,1)S(1)}, u32[]{:S(2)}, u32[]{:S(2)}) collective-permute-start(bf16[128,512]{1,0:T(8,128)(2,1)S(1)} %add_convert_fusion.7), channel_id=1, source_target_pairs={{0,16},{8,24},{16,0},{24,8},{1,17},{9,25},{17,1},{25,9},{2,18},{10... | collective-permute-start | bytes 393224 | tf_op jit(solution)/shard_map/ppermute | solution.py:383
  332.0 9.4 %collective-permute-start.40 = (bf16[128,1024]{1,0:T(8,128)(2,1)}, bf16[128,1024]{1,0:T(8,128)(2,1)S(1)}, u32[]{:S(2)}, u32[]{:S(2)}) collective-permute-start(bf16[128,1024]{1,0:T(8,128)(2,1)} %collective-permute-done.38), channel_id=1, source_target_pairs={{0,1},{1,0},{2,3},{3,2},{4,5},{5,4},{6,7},{7,6},{8,9},{9,8},{10,11... | collective-permute-start | bytes 786440 | tf_op jit(solution)/shard_map/ppermute | solution.py:112
  335.2 9.2 %collective-permute-start.41 = (bf16[128,1024]{1,0:T(8,128)(2,1)S(1)}, bf16[128,1024]{1,0:T(8,128)(2,1)S(1)}, u32[]{:S(2)}, u32[]{:S(2)}) collective-permute-start(bf16[128,1024]{1,0:T(8,128)(2,1)S(1)} %collective-permute-done.37), channel_id=1, source_target_pairs={{0,2},{1,3},{2,0},{3,1},{4,6},{5,7},{6,4},{7,5},{8,10},{9,11},{10,... | collective-permute-start | bytes 786440 | tf_op jit(solution)/shard_map/ppermute | solution.py:112
  336.7 13.1 %collective-permute-start.46 = (bf16[128,1024]{1,0:T(8,128)(2,1)}, bf16[128,1024]{1,0:T(8,128)(2,1)S(1)}, u32[]{:S(2)}, u32[]{:S(2)}) collective-permute-start(bf16[128,1024]{1,0:T(8,128)(2,1)} %collective-permute-done.44), channel_id=1, source_target_pairs={{0,1},{1,0},{2,3},{3,2},{4,5},{5,4},{6,7},{7,6},{8,9},{9,8},{10,11... | collective-permute-start | bytes 786440 | tf_op jit(solution)/shard_map/ppermute | solution.py:112
  339.0 10.9 %collective-permute-start.47 = (bf16[128,1024]{1,0:T(8,128)(2,1)}, bf16[128,1024]{1,0:T(8,128)(2,1)}, u32[]{:S(2)}, u32[]{:S(2)}) collective-permute-start(bf16[128,1024]{1,0:T(8,128)(2,1)} %collective-permute-done.43), channel_id=1, source_target_pairs={{0,2},{1,3},{2,0},{3,1},{4,6},{5,7},{6,4},{7,5},{8,10},{9,11},{10,... | collective-permute-start | bytes 786440 | tf_op jit(solution)/shard_map/ppermute | solution.py:112
  (124 other events, 1174.8 us)
